TPU v7x, 512 devices: a whole 4x8x8 slice. The times are simulated.
512 devices in a mesh: img: 8 (over x, core), sp: 64 (over y, z).
Axes of the slice: x: 4, y: 8, z: 8, core: 2. Of those that a mesh axis runs over, the one named last changes fastest.
Arguments:
- tokens: bfloat16 [8, 64, 16, 16, 768], P('img', 'sp'), may hold values from -6 to 6
- w_qkv: bfloat16 [768, 1152], P('img'), may hold values from -0.21875 to 0.21875
- score_scale: float32 [6], replicated, may hold values from 5 to 20
- grad_out: bfloat16 [8, 64, 16, 16, 384], P('img', 'sp'), may hold values from -1.75 to 1.75
Outputs:
- attended: bfloat16 [8, 64, 16, 16, 384], P('img', 'sp')
- grad_tokens: bfloat16 [8, 64, 16, 16, 768], P('img', 'sp')
- weight_grad: float32 [768, 1152], P('img', 'sp')
All inputs are finite; a program needn't handle non-finite values.
Results may differ from a plain program's by a relative error of at most 0.018.
Values may be sent and summed in bfloat16 or wider, within the bound.
A program may use at most 64 MiB of HBM per device.

v0:
```python
import math

import jax
import jax.numpy as jnp
from jax import lax
from jax.sharding import PartitionSpec as P

GRID = 128
COLS = 128
RADIUS = 3


norm_eps = 1e-06


def passed_along(x, axis, by):
    peers = lax.axis_size(axis)
    pairs = [(i, i + by) for i in range(peers) if 0 <= i + by < peers]
    return lax.ppermute(x, axis, pairs)


def block_pass(
    query_block, kv_block, grad_block, row_first, col_first, scales, radius, grid_rows, grid_cols
):
    local_rows, local_cols, width = query_block.shape
    heads = scales.shape[0]
    head_size = width // heads
    ext_rows = kv_block.shape[0]
    ext_cols = kv_block.shape[1]
    query_flat = query_block.reshape(local_rows * local_cols, width).astype(jnp.float32)
    kv_flat = kv_block.reshape(ext_rows * ext_cols, 2 * width)
    key_flat = kv_flat[:, :width].astype(jnp.float32)
    value_flat = kv_flat[:, width:]
    grad_flat = grad_block.reshape(local_rows * local_cols, width)
    query_pos = jnp.arange(local_rows * local_cols, dtype=jnp.int32)
    key_pos = jnp.arange(ext_rows * ext_cols, dtype=jnp.int32)
    query_row = (query_pos // local_cols)[:, None]
    query_col = (query_pos % local_cols)[:, None]
    key_row = (key_pos // ext_cols)[None, :]
    key_col = (key_pos % ext_cols)[None, :]
    global_row = row_first + key_row - radius
    global_col = col_first + key_col - radius
    allowed = (jnp.abs(key_row - radius - query_row) <= radius) & (
        jnp.abs(key_col - radius - query_col) <= radius
    )
    allowed = (
        allowed
        & (global_row >= 0)
        & (global_row < grid_rows)
        & (global_col >= 0)
        & (global_col < grid_cols)
    )
    scale_root = 1.0 / math.sqrt(head_size)
    outputs, query_grads, key_grads, value_grads = ([], [], [], [])
    for head_index in range(heads):
        lower = head_index * head_size
        upper = lower + head_size
        query_head = query_flat[:, lower:upper]
        key_head = key_flat[:, lower:upper]
        value_head = value_flat[:, lower:upper]
        grad_head = grad_flat[:, lower:upper]
        query_inv = (
            lax.rsqrt(jnp.mean(query_head * query_head, axis=-1, keepdims=True) + norm_eps)
            * scale_root
        )
        key_inv = (
            lax.rsqrt(jnp.mean(key_head * key_head, axis=-1, keepdims=True) + norm_eps) * scale_root
        )
        query_unit = (query_head * query_inv).astype(jnp.bfloat16)
        key_unit = (key_head * key_inv).astype(jnp.bfloat16)
        scores = scales[head_index] * lax.dot_general(
            query_unit, key_unit, (((1,), (1,)), ((), ())), preferred_element_type=jnp.float32
        )
        raised = jnp.where(allowed, jnp.exp(scores), jnp.zeros_like(scores))
        attention = raised / jnp.sum(raised, axis=-1, keepdims=True)
        attention_low = attention.astype(jnp.bfloat16)
        outputs.append(jnp.dot(attention_low, value_head, preferred_element_type=jnp.float32))
        value_grads.append(
            lax.dot_general(
                attention_low,
                grad_head,
                (((0,), (0,)), ((), ())),
                preferred_element_type=jnp.float32,
            )
        )
        grad_attention = lax.dot_general(
            grad_head, value_head, (((1,), (1,)), ((), ())), preferred_element_type=jnp.float32
        )
        row_total = jnp.sum(attention * grad_attention, axis=-1, keepdims=True)
        grad_scores = (scales[head_index] * attention * (grad_attention - row_total)).astype(
            jnp.bfloat16
        )
        grad_qunit = jnp.dot(grad_scores, key_unit, preferred_element_type=jnp.float32)
        grad_kunit = lax.dot_general(
            grad_scores, query_unit, (((0,), (0,)), ((), ())), preferred_element_type=jnp.float32
        )
        query_grads.append(
            query_inv
            * (
                grad_qunit
                - query_head
                * (query_inv * query_inv * head_size)
                * jnp.mean(grad_qunit * query_head, axis=-1, keepdims=True)
            )
        )
        key_grads.append(
            key_inv
            * (
                grad_kunit
                - key_head
                * (key_inv * key_inv * head_size)
                * jnp.mean(grad_kunit * key_head, axis=-1, keepdims=True)
            )
        )
    attended = (
        jnp.concatenate(outputs, axis=-1)
        .astype(jnp.bfloat16)
        .reshape(local_rows, local_cols, width)
    )
    query_grad = jnp.concatenate(query_grads, axis=-1).reshape(local_rows, local_cols, width)
    kv_grad = jnp.concatenate(key_grads + value_grads, axis=-1).reshape(
        ext_rows, ext_cols, 2 * width
    )
    return (attended, query_grad, kv_grad)


def own_span(step, size, reach):
    if step < 0:
        return (size - reach, size)
    if step > 0:
        return (0, reach)
    return (0, size)


def ext_span(step, size, reach):
    if step < 0:
        return (0, reach)
    if step > 0:
        return (reach + size, 2 * reach + size)
    return (reach, reach + size)


def local(tokens, w_qkv, score_scale, grad_out):
    images, tile_one, local_rows, local_cols, model_width = tokens.shape
    triple = w_qkv.shape[1]
    width = triple // 3
    token_count = images * local_rows * local_cols
    col_tiles = COLS // local_cols
    flat_tokens = tokens.reshape(token_count, model_width)
    full_weights = lax.all_gather(w_qkv, "img", axis=0, tiled=True)
    projected = jnp.dot(flat_tokens, full_weights, preferred_element_type=jnp.float32)
    qkv = projected.astype(jnp.bfloat16).reshape(images, local_rows, local_cols, triple)
    queries = qkv[..., :width]
    kv_own = qkv[..., width:]
    ext_rows = local_rows + 2 * RADIUS
    ext_cols = local_cols + 2 * RADIUS
    neighbours = [
        (row_step, col_step)
        for row_step in (-1, 0, 1)
        for col_step in (-1, 0, 1)
        if row_step != 0 or col_step != 0
    ]
    extended = jnp.zeros((images, ext_rows, ext_cols, 2 * width), jnp.bfloat16)
    extended = extended.at[:, RADIUS : RADIUS + local_rows, RADIUS : RADIUS + local_cols].set(
        kv_own
    )
    for row_step, col_step in neighbours:
        row_low, row_high = own_span(row_step, local_rows, RADIUS)
        col_low, col_high = own_span(col_step, local_cols, RADIUS)
        slab = kv_own[:, row_low:row_high, col_low:col_high]
        arrived = passed_along(slab, "sp", -(row_step * col_tiles + col_step))
        erow_low, erow_high = ext_span(row_step, local_rows, RADIUS)
        ecol_low, ecol_high = ext_span(col_step, local_cols, RADIUS)
        extended = extended.at[:, erow_low:erow_high, ecol_low:ecol_high].set(arrived)
    tile_index = lax.axis_index("sp")
    row_first = tile_index // col_tiles * local_rows
    col_first = tile_index % col_tiles * local_cols
    attended_list, query_list, kv_list = ([], [], [])
    attended_one, query_one, kv_one = block_pass(
        queries[0],
        extended[0],
        grad_out[0, 0],
        row_first,
        col_first,
        score_scale,
        RADIUS,
        GRID,
        COLS,
    )
    attended_list.append(attended_one)
    query_list.append(query_one)
    kv_list.append(kv_one)
    attended = jnp.stack(attended_list, axis=0)
    query_grad = jnp.stack(query_list, axis=0)
    kv_grad = jnp.stack(kv_list, axis=0)
    owned = kv_grad[:, RADIUS : RADIUS + local_rows, RADIUS : RADIUS + local_cols]
    for row_step, col_step in neighbours:
        erow_low, erow_high = ext_span(row_step, local_rows, RADIUS)
        ecol_low, ecol_high = ext_span(col_step, local_cols, RADIUS)
        returned = kv_grad[:, erow_low:erow_high, ecol_low:ecol_high]
        arrived = passed_along(
            returned.astype(jnp.bfloat16), "sp", row_step * col_tiles + col_step
        ).astype(returned.dtype)
        row_low, row_high = own_span(row_step, local_rows, RADIUS)
        col_low, col_high = own_span(col_step, local_cols, RADIUS)
        owned = owned.at[:, row_low:row_high, col_low:col_high].add(arrived)
    grad_qkv = (
        jnp.concatenate([query_grad, owned], axis=-1)
        .astype(jnp.bfloat16)
        .reshape(token_count, triple)
    )
    grad_flat = lax.dot_general(
        grad_qkv, full_weights, (((1,), (1,)), ((), ())), preferred_element_type=jnp.float32
    )
    grad_tokens = grad_flat.astype(jnp.bfloat16).reshape(
        images, 1, local_rows, local_cols, model_width
    )
    image_total = lax.axis_size("img") * images
    partial_columns = lax.psum_scatter(
        lax.dot_general(
            grad_qkv, flat_tokens, (((0,), (0,)), ((), ())), preferred_element_type=jnp.float32
        ),
        "sp",
        scatter_dimension=0,
        tiled=True,
    )
    weight_grad = (
        lax.psum_scatter(
            partial_columns.astype(jnp.bfloat16), "img", scatter_dimension=1, tiled=True
        )
        .astype(jnp.float32)
        .T
    )
    return (
        attended.reshape(images, 1, local_rows, local_cols, width),
        grad_tokens,
        weight_grad / image_total,
    )


def solution(mesh):
    return jax.shard_map(
        local,
        mesh=mesh,
        in_specs=(
            P("img", "sp", None, None, None),
            P("img", None),
            P(),
            P("img", "sp", None, None, None),
        ),
        out_specs=(
            P("img", "sp", None, None, None),
            P("img", "sp", None, None, None),
            P("img", "sp"),
        ),
        check_vma=False,
    )
```

profile of v0, /device:TPU:1, one launch (start us, length us, event | category | flops | bytes accessed | tf_op | source)
XLA Modules:
  0.0 534.3 jit_solution(12251805753063657733)
XLA Ops:
  11.8 1.4 and_reduce_fusion.2
  13.2 1.4 and_reduce_fusion.1
  14.6 1.4 and_reduce_fusion
  16.1 1.5 fusion.86
  17.6 28.6 %all-gather.2.cloned.1.call-done = bf16[768,1152]{1,0:T(8,128)(2,1)} async-done(((bf16[96,1152]{1,0:T(8,128)(2,1)}), bf16[768,1152]{1,0:T(8,128)(2,1)}) %all-gather.2.cloned.1.call-update) | async-done | bytes 1769488 | tf_op jit(solution)/shard_map/all_gather | solution.py:150
  46.2 2.2 convolution_convert_fusion
  48.6 4.0 collective-permute-start
  52.6 3.1 collective-permute-start.1
  55.7 4.1 collective-permute-start.2
  59.9 2.1 collective-permute-start.3
  68.5 1.9 dynamic-slice_select_fusion
  70.4 1.7 scatter.34
  72.1 1.5 collective-permute-start.7
  73.6 1.9 dynamic-slice_select_fusion.1
  75.5 1.5 scatter.35
  77.0 2.6 scatter.36
  79.6 1.8 scatter.39
  106.7 1.4 multiply_reduce_fusion.19
  108.9 1.4 multiply_reduce_fusion.18
  119.2 1.5 copy.54
  124.6 5.4 %collective-permute-start.12 = (bf16[1,16,3,768]{3,2,1,0:T(4,128)(2,1)}, bf16[1,16,3,768]{3,2,1,0:T(4,128)(2,1)}, u32[]{:S(2)}, u32[]{:S(2)}) collective-permute-start(bf16[1,16,3,768]{3,2,1,0:T(4,128)(2,1)} %get-tuple-element.229), channel_id=1, source_target_pairs={{0,1},{1,2},{2,3},{3,4},{4,5},{5,6},{6,7},{7,8},{8,9},{9,10},{10,1... | collective-permute-start | bytes 221192 | tf_op jit(solution)/shard_map/ppermute | solution.py:19
  130.8 10.6 %collective-permute-start.13 = (bf16[1,3,3,768]{3,2,1,0:T(4,128)(2,1)}, bf16[1,3,3,768]{3,2,1,0:T(4,128)(2,1)S(1)}, u32[]{:S(2)}, u32[]{:S(2)}) collective-permute-start(bf16[1,3,3,768]{3,2,1,0:T(4,128)(2,1)} %get-tuple-element.224), channel_id=1, source_target_pairs={{0,7},{1,8},{2,9},{3,10},{4,11},{5,12},{6,13},{7,14},{8,15},{9,16}... | collective-permute-start | bytes 41480 | tf_op jit(solution)/shard_map/ppermute | solution.py:19
  142.4 7.0 %collective-permute-start.14 = (bf16[1,3,16,768]{3,2,1,0:T(8,128)(2,1)}, bf16[1,3,16,768]{3,2,1,0:T(8,128)(2,1)S(1)}, u32[]{:S(2)}, u32[]{:S(2)}) collective-permute-start(bf16[1,3,16,768]{3,2,1,0:T(8,128)(2,1)} %get-tuple-element.227), channel_id=1, source_target_pairs={{0,8},{1,9},{2,10},{3,11},{4,12},{5,13},{6,14},{7,15},{8,16},{9,17... | collective-permute-start | bytes 221192 | tf_op jit(solution)/shard_map/ppermute | solution.py:19
  150.4 3.0 collective-permute-start.15
  154.8 2.2 scatter-add.31
  157.9 3.4 scatter-add.34
  161.3 2.0 add_select_fusion
  163.3 1.5 scatter-add.35
  165.6 2.4 fusion.95
  168.1 268.0 %all-reduce.3 = bf16[1152,768]{1,0:T(8,128)(2,1)S(1)} all-reduce(f32[1152,768]{1,0:T(8,128)} %fusion.95), channel_id=2, replica_groups=mesh['img'=8,'sp'=64] {'sp'}, use_global_device_ids=true, to_apply=%region_39.40.clone | all-reduce | flops 884736 | bytes 5308416
  437.0 2.9 convolution_convert_fusion.1
  439.9 86.1 %reduce-scatter.4.cloned.1.call-done = bf16[96,18]{1,0:T(8,128)(2,1)} async-done(((bf16[768,18]{1,0:T(8,128)(2,1)}), bf16[96,18]{1,0:T(8,128)(2,1)}) %reduce-scatter.4.cloned.1.call-update) | async-done | bytes 3472
  (247 shorter events, 56.5 us)
Async XLA Ops:
  7.2 39.1 %copy-start = (bf16[1,1,16,16,768]{4,3,2,1,0:T(8,128)(2,1)S(1)}, bf16[1,1,16,16,768]{4,3,2,1,0:T(8,128)(2,1)}, u32[]{:S(2)}) copy-start(bf16[1,1,16,16,768]{4,3,2,1,0:T(8,128)(2,1)} %param.38) | copy-start | bytes 1179652
  7.2 39.0 %all-gather.2.cloned.1.call-start = ((), (), s32[]{:S(2)}) async-start(), calls=%async_computation.1 | async-start | bytes 1990656 | tf_op jit(solution)/shard_map/all_gather | solution.py:150
  7.9 518.1 %reduce-scatter.4.cloned.1.call-start = ((), (), s32[]{:S(2)}) async-start(), calls=%async_computation.2 | async-start | bytes 221184
  48.6 17.1 %collective-permute-start = (bf16[1,3,3,768]{3,2,1,0:T(4,128)(2,1)S(1)}, bf16[1,3,3,768]{3,2,1,0:T(4,128)(2,1)S(1)}, u32[]{:S(2)}, u32[]{:S(2)}) collective-permute-start(bf16[1,3,3,768]{3,2,1,0:T(4,128)(2,1)S(1)} %get-tuple-element.234), channel_id=1, source_target_pairs={{0,9},{1,10},{2,11},{3,12},{4,13},{5,14},{6,15},{7,16},{8,17},{9,1... | collective-permute-start | bytes 41480 | tf_op jit(solution)/shard_map/ppermute | solution.py:19
  52.6 14.6 %collective-permute-start.1 = (bf16[1,3,16,768]{3,2,1,0:T(8,128)(2,1)S(1)}, bf16[1,3,16,768]{3,2,1,0:T(8,128)(2,1)S(1)}, u32[]{:S(2)}, u32[]{:S(2)}) collective-permute-start(bf16[1,3,16,768]{3,2,1,0:T(8,128)(2,1)S(1)} %get-tuple-element.236), channel_id=1, source_target_pairs={{0,8},{1,9},{2,10},{3,11},{4,12},{5,13},{6,14},{7,15},{8,16},{9,17... | collective-permute-start | bytes 221192 | tf_op jit(solution)/shard_map/ppermute | solution.py:19
  55.7 16.4 %collective-permute-start.2 = (bf16[1,3,3,768]{3,2,1,0:T(4,128)(2,1)S(1)}, bf16[1,3,3,768]{3,2,1,0:T(4,128)(2,1)S(1)}, u32[]{:S(2)}, u32[]{:S(2)}) collective-permute-start(bf16[1,3,3,768]{3,2,1,0:T(4,128)(2,1)S(1)} %get-tuple-element.233), channel_id=1, source_target_pairs={{0,7},{1,8},{2,9},{3,10},{4,11},{5,12},{6,13},{7,14},{8,15},{9,16}... | collective-permute-start | bytes 41480 | tf_op jit(solution)/shard_map/ppermute | solution.py:19
  59.9 17.2 %collective-permute-start.3 = (bf16[1,16,3,768]{3,2,1,0:T(4,128)(2,1)S(1)}, bf16[1,16,3,768]{3,2,1,0:T(4,128)(2,1)S(1)}, u32[]{:S(2)}, u32[]{:S(2)}) collective-permute-start(bf16[1,16,3,768]{3,2,1,0:T(4,128)(2,1)S(1)} %get-tuple-element.238), channel_id=1, source_target_pairs={{0,1},{1,2},{2,3},{3,4},{4,5},{5,6},{6,7},{7,8},{8,9},{9,10},{10,1... | collective-permute-start | bytes 221192 | tf_op jit(solution)/shard_map/ppermute | solution.py:19
  61.9 17.7 %collective-permute-start.4 = (bf16[1,16,3,768]{3,2,1,0:T(4,128)(2,1)S(1)}, bf16[1,16,3,768]{3,2,1,0:T(4,128)(2,1)S(1)}, u32[]{:S(2)}, u32[]{:S(2)}) collective-permute-start(bf16[1,16,3,768]{3,2,1,0:T(4,128)(2,1)S(1)} %get-tuple-element.237), channel_id=1, source_target_pairs={{1,0},{2,1},{3,2},{4,3},{5,4},{6,5},{7,6},{8,7},{9,8},{10,9},{11,1... | collective-permute-start | bytes 221192 | tf_op jit(solution)/shard_map/ppermute | solution.py:19
  63.6 35.4 %copy-start.11 = (f32[256,64]{0,1:T(8,128)}, f32[256,64]{0,1:T(8,128)S(1)}, u32[]{:S(2)}) copy-start(f32[256,64]{0,1:T(8,128)S(1)} %copy.57) | copy-start | bytes 196612
  63.7 37.5 %copy-start.9 = (f32[256,64]{0,1:T(8,128)}, f32[256,64]{0,1:T(8,128)S(1)}, u32[]{:S(2)}) copy-start(f32[256,64]{0,1:T(8,128)S(1)} %copy.59) | copy-start | bytes 196612
  63.8 39.7 %copy-start.7 = (f32[256,64]{0,1:T(8,128)}, f32[256,64]{0,1:T(8,128)S(1)}, u32[]{:S(2)}) copy-start(f32[256,64]{0,1:T(8,128)S(1)} %copy.60) | copy-start | bytes 196612
  64.0 41.8 %copy-start.5 = (f32[256,64]{0,1:T(8,128)}, f32[256,64]{0,1:T(8,128)S(1)}, u32[]{:S(2)}) copy-start(f32[256,64]{0,1:T(8,128)S(1)} %copy.61) | copy-start | bytes 196612
  64.1 44.0 %copy-start.1 = (f32[256,64]{0,1:T(8,128)}, f32[256,64]{0,1:T(8,128)S(1)}, u32[]{:S(2)}) copy-start(f32[256,64]{0,1:T(8,128)S(1)} %copy.62) | copy-start | bytes 196612
  64.8 45.5 %copy-start.3 = (f32[256,64]{0,1:T(8,128)}, f32[256,64]{0,1:T(8,128)S(1)}, u32[]{:S(2)}) copy-start(f32[256,64]{0,1:T(8,128)S(1)} %copy.63) | copy-start | bytes 196612
  65.4 44.9 %copy-start.26 = (f32[256]{0:T(256)}, f32[256]{0:T(256)S(1)}, u32[]{:S(2)}) copy-start(f32[256]{0:T(256)S(1)} %get-tuple-element.258) | copy-start | bytes 3076
  65.6 15.9 %collective-permute-start.5 = (bf16[1,3,3,768]{3,2,1,0:T(4,128)(2,1)S(1)}, bf16[1,3,3,768]{3,2,1,0:T(4,128)(2,1)S(1)}, u32[]{:S(2)}, u32[]{:S(2)}) collective-permute-start(bf16[1,3,3,768]{3,2,1,0:T(4,128)(2,1)S(1)} %get-tuple-element.232), channel_id=1, source_target_pairs={{7,0},{8,1},{9,2},{10,3},{11,4},{12,5},{13,6},{14,7},{15,8},{16,9}... | collective-permute-start | bytes 41480 | tf_op jit(solution)/shard_map/ppermute | solution.py:19
  67.2 14.6 %collective-permute-start.6 = (bf16[1,3,16,768]{3,2,1,0:T(8,128)(2,1)S(1)}, bf16[1,3,16,768]{3,2,1,0:T(8,128)(2,1)S(1)}, u32[]{:S(2)}, u32[]{:S(2)}) collective-permute-start(bf16[1,3,16,768]{3,2,1,0:T(8,128)(2,1)S(1)} %get-tuple-element.235), channel_id=1, source_target_pairs={{8,0},{9,1},{10,2},{11,3},{12,4},{13,5},{14,6},{15,7},{16,8},{17,9... | collective-permute-start | bytes 221192 | tf_op jit(solution)/shard_map/ppermute | solution.py:19
  72.1 10.0 %collective-permute-start.7 = (bf16[1,3,3,768]{3,2,1,0:T(4,128)(2,1)S(1)}, bf16[1,3,3,768]{3,2,1,0:T(4,128)(2,1)S(1)}, u32[]{:S(2)}, u32[]{:S(2)}) collective-permute-start(bf16[1,3,3,768]{3,2,1,0:T(4,128)(2,1)S(1)} %get-tuple-element.231), channel_id=1, source_target_pairs={{9,0},{10,1},{11,2},{12,3},{13,4},{14,5},{15,6},{16,7},{17,8},{18,... | collective-permute-start | bytes 41480 | tf_op jit(solution)/shard_map/ppermute | solution.py:19
  113.1 3.9 copy-start.2
  113.1 3.9 copy-start.4
  113.1 3.9 copy-start.18
  113.1 3.9 copy-start.27
  113.2 3.9 copy-start.29
  115.5 15.3 %collective-permute-start.8 = (bf16[1,3,3,768]{3,2,1,0:T(4,128)(2,1)}, bf16[1,3,3,768]{3,2,1,0:T(4,128)(2,1)}, u32[]{:S(2)}, u32[]{:S(2)}) collective-permute-start(bf16[1,3,3,768]{3,2,1,0:T(4,128)(2,1)} %get-tuple-element.226), channel_id=1, source_target_pairs={{9,0},{10,1},{11,2},{12,3},{13,4},{14,5},{15,6},{16,7},{17,8},{18,... | collective-permute-start | bytes 41480 | tf_op jit(solution)/shard_map/ppermute | solution.py:19
  120.7 21.7 %collective-permute-start.9 = (bf16[1,3,16,768]{3,2,1,0:T(8,128)(2,1)}, bf16[1,3,16,768]{3,2,1,0:T(8,128)(2,1)}, u32[]{:S(2)}, u32[]{:S(2)}) collective-permute-start(bf16[1,3,16,768]{3,2,1,0:T(8,128)(2,1)} %get-tuple-element.228), channel_id=1, source_target_pairs={{8,0},{9,1},{10,2},{11,3},{12,4},{13,5},{14,6},{15,7},{16,8},{17,9... | collective-permute-start | bytes 221192 | tf_op jit(solution)/shard_map/ppermute | solution.py:19
  122.0 28.4 %collective-permute-start.10 = (bf16[1,3,3,768]{3,2,1,0:T(4,128)(2,1)}, bf16[1,3,3,768]{3,2,1,0:T(4,128)(2,1)S(1)}, u32[]{:S(2)}, u32[]{:S(2)}) collective-permute-start(bf16[1,3,3,768]{3,2,1,0:T(4,128)(2,1)} %get-tuple-element.225), channel_id=1, source_target_pairs={{7,0},{8,1},{9,2},{10,3},{11,4},{12,5},{13,6},{14,7},{15,8},{16,9}... | collective-permute-start | bytes 41480 | tf_op jit(solution)/shard_map/ppermute | solution.py:19
  123.3 30.5 %collective-permute-start.11 = (bf16[1,16,3,768]{3,2,1,0:T(4,128)(2,1)}, bf16[1,16,3,768]{3,2,1,0:T(4,128)(2,1)}, u32[]{:S(2)}, u32[]{:S(2)}) collective-permute-start(bf16[1,16,3,768]{3,2,1,0:T(4,128)(2,1)} %get-tuple-element.230), channel_id=1, source_target_pairs={{1,0},{2,1},{3,2},{4,3},{5,4},{6,5},{7,6},{8,7},{9,8},{10,9},{11,1... | collective-permute-start | bytes 221192 | tf_op jit(solution)/shard_map/ppermute | solution.py:19
  124.6 32.4 %collective-permute-start.12 = (bf16[1,16,3,768]{3,2,1,0:T(4,128)(2,1)}, bf16[1,16,3,768]{3,2,1,0:T(4,128)(2,1)}, u32[]{:S(2)}, u32[]{:S(2)}) collective-permute-start(bf16[1,16,3,768]{3,2,1,0:T(4,128)(2,1)} %get-tuple-element.229), channel_id=1, source_target_pairs={{0,1},{1,2},{2,3},{3,4},{4,5},{5,6},{6,7},{7,8},{8,9},{9,10},{10,1... | collective-permute-start | bytes 221192 | tf_op jit(solution)/shard_map/ppermute | solution.py:19
  130.8 30.5 %collective-permute-start.13 = (bf16[1,3,3,768]{3,2,1,0:T(4,128)(2,1)}, bf16[1,3,3,768]{3,2,1,0:T(4,128)(2,1)S(1)}, u32[]{:S(2)}, u32[]{:S(2)}) collective-permute-start(bf16[1,3,3,768]{3,2,1,0:T(4,128)(2,1)} %get-tuple-element.224), channel_id=1, source_target_pairs={{0,7},{1,8},{2,9},{3,10},{4,11},{5,12},{6,13},{7,14},{8,15},{9,16}... | collective-permute-start | bytes 41480 | tf_op jit(solution)/shard_map/ppermute | solution.py:19
  142.4 22.4 %collective-permute-start.14 = (bf16[1,3,16,768]{3,2,1,0:T(8,128)(2,1)}, bf16[1,3,16,768]{3,2,1,0:T(8,128)(2,1)S(1)}, u32[]{:S(2)}, u32[]{:S(2)}) collective-permute-start(bf16[1,3,16,768]{3,2,1,0:T(8,128)(2,1)} %get-tuple-element.227), channel_id=1, source_target_pairs={{0,8},{1,9},{2,10},{3,11},{4,12},{5,13},{6,14},{7,15},{8,16},{9,17... | collective-permute-start | bytes 221192 | tf_op jit(solution)/shard_map/ppermute | solution.py:19
  150.4 14.5 %collective-permute-start.15 = (bf16[1,3,3,768]{3,2,1,0:T(4,128)(2,1)}, bf16[1,3,3,768]{3,2,1,0:T(4,128)(2,1)S(1)}, u32[]{:S(2)}, u32[]{:S(2)}) collective-permute-start(bf16[1,3,3,768]{3,2,1,0:T(4,128)(2,1)} %get-tuple-element.223), channel_id=1, source_target_pairs={{0,9},{1,10},{2,11},{3,12},{4,13},{5,14},{6,15},{7,16},{8,17},{9,1... | collective-permute-start | bytes 41480 | tf_op jit(solution)/shard_map/ppermute | solution.py:19
  154.7 10.5 %copy-start.19 = (bf16[256,64]{1,0:T(8,128)(2,1)S(1)}, bf16[256,64]{1,0:T(8,128)(2,1)}, u32[]{:S(2)}) copy-start(bf16[256,64]{1,0:T(8,128)(2,1)} %copy.54) | copy-start | bytes 98308
  (22 other events, 72.1 us)
Sparse Core Ops, SparseCore 0:
  10.1 36.0 all-gather.1
  437.1 88.8 reduce-scatter.3
where the time goes:
time: 536 us; the launch traced here: 534 us
  blocking collectives  268 us (50%)
  waiting for transfers between devices  115 us (21%)
  starting transfers between devices  50 us (9%)
  matrix products  32.1 us (6%)
  local copies, waits for them, and re-layouts  31.3 us (6%)
  other arithmetic  21.2 us (4%)
  between operations  16.2 us (3%)
    unnamed x1, blocking collectives  268 us
    unnamed x3, waiting for transfers between devices  86.8 us
    ppermute x16, starting transfers between devices, passed_along(): return lax.ppermute(x, axis, pairs)  49.9 us
    all_gather x1, waiting for transfers between devices, local(): full_weights = lax.all_gather(w_qkv, 'img', axis=0, tiled=True)  28.6 us
    another operation x17, other arithmetic  10.9 us
  transfers between devices with their start and end apart: 18, of which 2 were waited for; matrix products, arithmetic and copies ran while one was open for 8% of the time, Pallas kernels for 0%

commit v1 on v0

--- a/solution.py
+++ b/solution.py
@@ -3,8 +3,13 @@
 import jax
 import jax.numpy as jnp
 from jax import lax
+from jax.experimental import pallas as pl
+from jax.experimental.pallas import tpu as pltpu
 from jax.sharding import PartitionSpec as P
 
+MESH = pl.DeviceIdType.MESH
+BF16 = jnp.bfloat16
+F32 = jnp.float32
 GRID = 128
 COLS = 128
 RADIUS = 3
@@ -139,6 +144,132 @@
         return (reach + size, 2 * reach + size)
     return (reach, reach + size)
 
+def remote(src, dst, send, recv, device):
+    return pltpu.make_async_remote_copy(
+        src_ref=src,
+        dst_ref=dst,
+        send_sem=send,
+        recv_sem=recv,
+        device_id=device,
+        device_id_type=MESH,
+    )
+
+
+def reduce_kernel(
+    tok_ref, gq_ref, out_ref,
+    tok_t, s1, r1, s2, r2, acc, acc_t, s3, r3, acc4, s4, r4, fin,
+    core_send, core_recv, x_send, x_recv, y_send, y_recv, z_send, z_recv,
+):
+    img = lax.axis_index("img")
+    sp = lax.axis_index("sp")
+    x, c = img // 2, img % 2
+    y, z = sp // 8, sp % 8
+    other_core = (2 * x + 1 - c, sp)
+    x_peer = [((2 * ((x + d) % 4) + c), sp) for d in range(4)]
+    y_peer = [(img, 8 * ((y + d) % 8) + z) for d in range(8)]
+    z_peer = [(img, 8 * y + (z + d) % 8) for d in range(8)]
+
+    barrier = pltpu.get_barrier_semaphore()
+    peers = [other_core] + x_peer[1:] + y_peer[1:] + z_peer[1:]
+    for peer in peers:
+        pl.semaphore_signal(barrier, inc=1, device_id=peer, device_id_type=MESH)
+
+    for b in range(8):
+        tok_t[b] = tok_ref[:, 96 * b : 96 * b + 96].astype(F32).T.astype(BF16)
+    acc[:, 96:128, :] = jnp.zeros((3, 32, 384), F32)
+    acc4[...] = jnp.zeros_like(acc4)
+    pl.semaphore_wait(barrier, len(peers))
+
+    def product(p, block):
+        return jnp.dot(tok_t[block], gq_ref[p], preferred_element_type=F32)
+
+    core_copies = []
+    for p in range(3):
+        for k in range(4):
+            s1[p, k] = product(p, 2 * k + 1 - c).astype(BF16)
+        copy = remote(s1.at[p], r1.at[p], core_send.at[p], core_recv.at[p], other_core)
+        copy.start()
+        core_copies.append(copy)
+    x_copies = []
+    for p in range(3):
+        core_copies[p].wait()
+        for d in range(1, 4):
+            to = (x + d) % 4
+            s2[p, d - 1] = (product(p, 2 * to + c) + r1[p, to].astype(F32)).astype(BF16)
+            copy = remote(
+                s2.at[p, d - 1], r2.at[p, d - 1], x_send.at[p, d - 1], x_recv.at[p, d - 1], x_peer[d]
+            )
+            copy.start()
+            x_copies.append(copy)
+        acc[p, 0:96] = product(p, img) + r1[p, x].astype(F32)
+    for p in range(3):
+        total = acc[p, 0:96]
+        for d in range(3):
+            x_copies[3 * p + d].wait()
+            total += r2[p, d].astype(F32)
+        acc[p, 0:96] = total
+        turned = acc[p].T
+        for part in range(3):
+            low = 384 * part + 128 * p
+            acc_t[low : low + 128] = turned[128 * part : 128 * part + 128]
+    y_copies = []
+    for d in range(1, 8):
+        to = (y + d) % 8
+        s3[d - 1] = acc_t[pl.ds(pl.multiple_of(144 * to, 16), 144)].astype(BF16)
+        copy = remote(s3.at[d - 1], r3.at[d - 1], y_send.at[d - 1], y_recv.at[d - 1], y_peer[d])
+        copy.start()
+        y_copies.append(copy)
+    total = acc_t[pl.ds(pl.multiple_of(144 * y, 16), 144)]
+    for d in range(7):
+        y_copies[d].wait()
+        total += r3[d].astype(F32)
+    acc4[0:144] = total
+    for g in range(8):
+        s4[g] = acc4[18 * g : 18 * g + 24]
+    z_copies = []
+    for d in range(1, 8):
+        copy = remote(
+            s4.at[(z + d) % 8], r4.at[d - 1], z_send.at[d - 1], z_recv.at[d - 1], z_peer[d]
+        )
+        copy.start()
+        z_copies.append(copy)
+    total = s4[z]
+    for d in range(7):
+        z_copies[d].wait()
+        total += r4[d]
+    fin[...] = jnp.zeros_like(fin)
+    fin[0:24] = total * (1.0 / 8.0)
+    out_ref[...] = fin[...].T[0:96, 0:18]
+
+
+def reduced_weight_grad(flat_tokens, grad_parts):
+    dma = pltpu.SemaphoreType.DMA
+    return pl.pallas_call(
+        reduce_kernel,
+        out_shape=jax.ShapeDtypeStruct((96, 18), F32),
+        in_specs=[pl.BlockSpec(memory_space=pltpu.VMEM)] * 2,
+        out_specs=pl.BlockSpec(memory_space=pltpu.VMEM),
+        scratch_shapes=[
+            pltpu.VMEM((8, 96, 256), BF16),
+            pltpu.VMEM((3, 4, 96, 384), BF16),
+            pltpu.VMEM((3, 4, 96, 384), BF16),
+            pltpu.VMEM((3, 3, 96, 384), BF16),
+            pltpu.VMEM((3, 3, 96, 384), BF16),
+            pltpu.VMEM((3, 128, 384), F32),
+            pltpu.VMEM((1152, 128), F32),
+            pltpu.VMEM((7, 144, 128), BF16),
+            pltpu.VMEM((7, 144, 128), BF16),
+            pltpu.VMEM((152, 128), F32),
+            pltpu.VMEM((8, 24, 128), F32),
+            pltpu.VMEM((7, 24, 128), F32),
+            pltpu.VMEM((128, 128), F32),
+            dma((3,)), dma((3,)), dma((3, 3)), dma((3, 3)), dma((7,)), dma((7,)), dma((7,)), dma((7,)),
+        ],
+        compiler_params=pltpu.CompilerParams(
+            collective_id=0, has_side_effects=True, vmem_limit_bytes=32 * 1024 * 1024
+        ),
+    )(flat_tokens, grad_parts)
+
 
 def local(tokens, w_qkv, score_scale, grad_out):
     images, tile_one, local_rows, local_cols, model_width = tokens.shape
@@ -215,26 +346,12 @@
     grad_tokens = grad_flat.astype(jnp.bfloat16).reshape(
         images, 1, local_rows, local_cols, model_width
     )
-    image_total = lax.axis_size("img") * images
-    partial_columns = lax.psum_scatter(
-        lax.dot_general(
-            grad_qkv, flat_tokens, (((0,), (0,)), ((), ())), preferred_element_type=jnp.float32
-        ),
-        "sp",
-        scatter_dimension=0,
-        tiled=True,
-    )
-    weight_grad = (
-        lax.psum_scatter(
-            partial_columns.astype(jnp.bfloat16), "img", scatter_dimension=1, tiled=True
-        )
-        .astype(jnp.float32)
-        .T
-    )
+    grad_parts = grad_qkv.reshape(token_count, 3, 3, 128).transpose(2, 0, 1, 3).reshape(3, token_count, 384)
+    weight_grad = reduced_weight_grad(flat_tokens, grad_parts)
     return (
         attended.reshape(images, 1, local_rows, local_cols, width),
         grad_tokens,
-        weight_grad / image_total,
+        weight_grad,
     )
 
 

time: 536 us -> 224 us (0.42)
  blocking collectives: 268 us -> 0 us
  waiting for transfers between devices: 115 us -> 31.4 us
  Pallas kernels: 0 us -> 41.9 us
    unnamed x1 -> x0, blocking collectives: 268 us -> none
    unnamed x3 -> x1, waiting for transfers between devices: 86.8 us -> 0.68 us
    pallas_call x0 -> x1, Pallas kernels: none -> 41.9 us  [reduced_weight_grad(): pl.pallas_call(reduce_kernel, out_shape=jax.ShapeDtypeStruct((96, 18), F3...]
    another operation x17 -> x11, other arithmetic: 10.9 us -> 10 us
  transfers between devices with their start and end apart: 18 -> 17, of which waited for: 2 -> 1; matrix products, arithmetic and copies ran while one was open for 8% -> 19% of each run, Pallas kernels for 0% -> 0%
where the time goes in v1:
time: 224 us; the launch traced here: 222 us
  starting transfers between devices  50 us (22%)
  Pallas kernels  41.9 us (19%)
  waiting for transfers between devices  31.4 us (14%)
  local copies, waits for them, and re-layouts  30.1 us (13%)
  matrix products  29.7 us (13%)
  other arithmetic  23 us (10%)
  between operations  15.5 us (7%)
    ppermute x16, starting transfers between devices, passed_along(): return lax.ppermute(x, axis, pairs)  49.9 us
    pallas_call x1, Pallas kernels, reduced_weight_grad(): pl.pallas_call(reduce_kernel, out_shape=jax.ShapeDtypeStruct((96, 18), F3...  41.9 us
    all_gather x1, waiting for transfers between devices, local(): full_weights = lax.all_gather(w_qkv, 'img', axis=0, tiled=True)  30.7 us
    another operation x11, other arithmetic  10 us
    scatter x8, local copies, waits for them, and re-layouts, local(): extended.at[:, erow_low:erow_high, ecol_low:ecol_high].set(arrived)  8.66 us
    dot_general x6, matrix products, block_pass(): jnp.dot(grad_scores, key_unit, preferred_element_type=jnp.float32)  8.1 us
    scatter-add x6, local copies, waits for them, and re-layouts, local(): owned = owned.at[:, row_low:row_high, col_low:col_high].add(arrived)  7.85 us
    dot_general x6, matrix products, block_pass(): lax.dot_general(query_unit, key_unit, (((1,), (1,)), ((), ())), preferred...  7.19 us
  transfers between devices with their start and end apart: 17, of which 1 were waited for; matrix products, arithmetic and copies ran while one was open for 19% of the time, Pallas kernels for 0%

profile of v1, /device:TPU:1, one launch (start us, length us, event | category | flops | bytes accessed | tf_op | source)
XLA Modules:
  0.0 221.6 jit_solution(4713223924193634873)
XLA Ops:
  9.8 1.4 and_reduce_fusion.2
  11.2 1.4 and_reduce_fusion.1
  12.6 1.4 and_reduce_fusion
  14.0 1.5 fusion.86
  15.5 30.7 %all-gather.2.cloned.1.call-done = bf16[768,1152]{1,0:T(8,128)(2,1)} async-done(((bf16[96,1152]{1,0:T(8,128)(2,1)}), bf16[768,1152]{1,0:T(8,128)(2,1)}) %all-gather.2.cloned.1.call-update) | async-done | bytes 1769488 | tf_op jit(solution)/shard_map/all_gather | solution.py:281
  46.2 2.3 %convolution_convert_fusion = bf16[256,1152]{1,0:T(8,128)(2,1)S(1)} fusion(bf16[256,768]{1,0:T(8,128)(2,1)} %bitcast.59, bf16[768,1152]{1,0:T(8,128)(2,1)} %all-gather.2.cloned.1.call-done), kind=kOutput, calls=%fused_computation | convolution fusion | flops 453279744 | bytes 2752512 | tf_op jit(solution)/shard_map/dot_general | solution.py:282
  48.7 4.0 %collective-permute-start = (bf16[1,3,3,768]{3,2,1,0:T(4,128)(2,1)S(1)}, bf16[1,3,3,768]{3,2,1,0:T(4,128)(2,1)S(1)}, u32[]{:S(2)}, u32[]{:S(2)}) collective-permute-start(bf16[1,3,3,768]{3,2,1,0:T(4,128)(2,1)S(1)} %get-tuple-element.252), channel_id=1, source_target_pairs={{0,9},{1,10},{2,11},{3,12},{4,13},{5,14},{6,15},{7,16},{8,17},{9,1... | collective-permute-start | bytes 41480 | tf_op jit(solution)/shard_map/ppermute | solution.py:24
  52.7 3.1 %collective-permute-start.1 = (bf16[1,3,16,768]{3,2,1,0:T(8,128)(2,1)S(1)}, bf16[1,3,16,768]{3,2,1,0:T(8,128)(2,1)S(1)}, u32[]{:S(2)}, u32[]{:S(2)}) collective-permute-start(bf16[1,3,16,768]{3,2,1,0:T(8,128)(2,1)S(1)} %get-tuple-element.254), channel_id=1, source_target_pairs={{0,8},{1,9},{2,10},{3,11},{4,12},{5,13},{6,14},{7,15},{8,16},{9,17... | collective-permute-start | bytes 221192 | tf_op jit(solution)/shard_map/ppermute | solution.py:24
  55.8 4.1 %collective-permute-start.2 = (bf16[1,3,3,768]{3,2,1,0:T(4,128)(2,1)S(1)}, bf16[1,3,3,768]{3,2,1,0:T(4,128)(2,1)S(1)}, u32[]{:S(2)}, u32[]{:S(2)}) collective-permute-start(bf16[1,3,3,768]{3,2,1,0:T(4,128)(2,1)S(1)} %get-tuple-element.251), channel_id=1, source_target_pairs={{0,7},{1,8},{2,9},{3,10},{4,11},{5,12},{6,13},{7,14},{8,15},{9,16}... | collective-permute-start | bytes 41480 | tf_op jit(solution)/shard_map/ppermute | solution.py:24
  60.0 2.1 collective-permute-start.3
  70.9 2.0 dynamic-slice_select_fusion
  72.9 1.7 scatter.34
  74.6 1.5 collective-permute-start.7
  76.1 1.9 dynamic-slice_select_fusion.1
  78.0 1.4 scatter.35
  79.4 2.6 %scatter.36 = bf16[1,22,22,768]{3,2,1,0:T(8,128)(2,1)S(1)} dynamic-update-slice(bf16[1,22,22,768]{3,2,1,0:T(8,128)(2,1)S(1)} %scatter.35, bf16[1,16,3,768]{3,2,1,0:T(4,128)(2,1)S(1)} %collective-permute-done.3, s32[]{:T(128)} %constant.576.clone.1, s32[]{:T(128)} %constant.581.clone.1, s32[]{:T(128)} %constant.576.clone.1, s32[]{:T(128)} %constant.576.clone.1) | dynamic-update-slice | bytes 147460 | tf_op jit(solution)/shard_map/scatter | solution.py:305
  82.0 1.8 scatter.39
  100.0 1.4 multiply_reduce_fusion.23
  102.3 1.4 multiply_reduce_fusion.22
  104.5 1.3 multiply_reduce_fusion.21
  106.7 1.3 multiply_reduce_fusion.20
  111.2 1.4 multiply_reduce_fusion.18
  126.3 5.5 %collective-permute-start.12 = (bf16[1,16,3,768]{3,2,1,0:T(4,128)(2,1)}, bf16[1,16,3,768]{3,2,1,0:T(4,128)(2,1)}, u32[]{:S(2)}, u32[]{:S(2)}) collective-permute-start(bf16[1,16,3,768]{3,2,1,0:T(4,128)(2,1)} %get-tuple-element.247), channel_id=1, source_target_pairs={{0,1},{1,2},{2,3},{3,4},{4,5},{5,6},{6,7},{7,8},{8,9},{9,10},{10,1... | collective-permute-start | bytes 221192 | tf_op jit(solution)/shard_map/ppermute | solution.py:24
  132.8 10.5 %collective-permute-start.13 = (bf16[1,3,3,768]{3,2,1,0:T(4,128)(2,1)}, bf16[1,3,3,768]{3,2,1,0:T(4,128)(2,1)S(1)}, u32[]{:S(2)}, u32[]{:S(2)}) collective-permute-start(bf16[1,3,3,768]{3,2,1,0:T(4,128)(2,1)} %get-tuple-element.242), channel_id=1, source_target_pairs={{0,7},{1,8},{2,9},{3,10},{4,11},{5,12},{6,13},{7,14},{8,15},{9,16}... | collective-permute-start | bytes 41480 | tf_op jit(solution)/shard_map/ppermute | solution.py:24
  144.3 7.0 %collective-permute-start.14 = (bf16[1,3,16,768]{3,2,1,0:T(8,128)(2,1)}, bf16[1,3,16,768]{3,2,1,0:T(8,128)(2,1)S(1)}, u32[]{:S(2)}, u32[]{:S(2)}) collective-permute-start(bf16[1,3,16,768]{3,2,1,0:T(8,128)(2,1)} %get-tuple-element.245), channel_id=1, source_target_pairs={{0,8},{1,9},{2,10},{3,11},{4,12},{5,13},{6,14},{7,15},{8,16},{9,17... | collective-permute-start | bytes 221192 | tf_op jit(solution)/shard_map/ppermute | solution.py:24
  152.3 3.0 %collective-permute-start.15 = (bf16[1,3,3,768]{3,2,1,0:T(4,128)(2,1)S(1)}, bf16[1,3,3,768]{3,2,1,0:T(4,128)(2,1)S(1)}, u32[]{:S(2)}, u32[]{:S(2)}) collective-permute-start(bf16[1,3,3,768]{3,2,1,0:T(4,128)(2,1)S(1)} %copy-done.12), channel_id=1, source_target_pairs={{0,9},{1,10},{2,11},{3,12},{4,13},{5,14},{6,15},{7,16},{8,17},{9,1... | collective-permute-start | bytes 41480 | tf_op jit(solution)/shard_map/ppermute | solution.py:24
  157.4 2.2 scatter-add.31
  160.5 3.4 %scatter-add.34 = f32[1,16,16,768]{3,2,1,0:T(8,128)S(1)} dynamic-update-slice(f32[1,16,16,768]{3,2,1,0:T(8,128)S(1)} %scatter-add.31, f32[1,16,3,768]{3,2,1,0:T(4,128)S(1)} %slice_add_fusion, s32[]{:T(128)} %constant.576.clone.1, s32[]{:T(128)} %constant.576.clone.1, s32[]{:T(128)} %constant.576.clone.1, s32[]{:T(128)} %constant.576.clone.1) | dynamic-update-slice | bytes 294916 | tf_op jit(solution)/shard_map/scatter-add | solution.py:337
  163.9 1.8 add_select_fusion
  165.8 1.4 scatter-add.35
  168.9 41.9 %shard_map.67 = f32[96,18]{1,0:T(8,128)S(1)} custom-call(bf16[256,768]{1,0:T(8,128)(2,1)S(1)} %bitcast.60, bf16[3,256,384]{2,1,0:T(8,128)(2,1)S(1)} %copy.38.gq_ref), custom_call_target="tpu_custom_call" | custom-call | tf_op jit(solution)/shard_map/pallas_call | solution.py:247
  211.8 2.9 %convolution_convert_fusion.1 = bf16[256,768]{1,0:T(8,128)(2,1)} fusion(bf16[256,1152]{1,0:T(8,128)(2,1)S(1)} %concatenate.105, bf16[768,1152]{1,0:T(8,128)(2,1)} %all-gather.2.cloned.1.call-done), kind=kOutput, calls=%fused_computation.1 | convolution fusion | flops 453181440 | bytes 2752512 | tf_op jit(solution)/shard_map/dot_general | solution.py:343
  (240 shorter events, 54.7 us)
Async XLA Ops:
  7.2 39.0 %all-gather.2.cloned.1.call-start = ((), (), s32[]{:S(2)}) async-start(), calls=%async_computation | async-start | bytes 1990656 | tf_op jit(solution)/shard_map/all_gather | solution.py:281
  48.7 19.4 %collective-permute-start = (bf16[1,3,3,768]{3,2,1,0:T(4,128)(2,1)S(1)}, bf16[1,3,3,768]{3,2,1,0:T(4,128)(2,1)S(1)}, u32[]{:S(2)}, u32[]{:S(2)}) collective-permute-start(bf16[1,3,3,768]{3,2,1,0:T(4,128)(2,1)S(1)} %get-tuple-element.252), channel_id=1, source_target_pairs={{0,9},{1,10},{2,11},{3,12},{4,13},{5,14},{6,15},{7,16},{8,17},{9,1... | collective-permute-start | bytes 41480 | tf_op jit(solution)/shard_map/ppermute | solution.py:24
  52.7 16.9 %collective-permute-start.1 = (bf16[1,3,16,768]{3,2,1,0:T(8,128)(2,1)S(1)}, bf16[1,3,16,768]{3,2,1,0:T(8,128)(2,1)S(1)}, u32[]{:S(2)}, u32[]{:S(2)}) collective-permute-start(bf16[1,3,16,768]{3,2,1,0:T(8,128)(2,1)S(1)} %get-tuple-element.254), channel_id=1, source_target_pairs={{0,8},{1,9},{2,10},{3,11},{4,12},{5,13},{6,14},{7,15},{8,16},{9,17... | collective-permute-start | bytes 221192 | tf_op jit(solution)/shard_map/ppermute | solution.py:24
  55.8 18.8 %collective-permute-start.2 = (bf16[1,3,3,768]{3,2,1,0:T(4,128)(2,1)S(1)}, bf16[1,3,3,768]{3,2,1,0:T(4,128)(2,1)S(1)}, u32[]{:S(2)}, u32[]{:S(2)}) collective-permute-start(bf16[1,3,3,768]{3,2,1,0:T(4,128)(2,1)S(1)} %get-tuple-element.251), channel_id=1, source_target_pairs={{0,7},{1,8},{2,9},{3,10},{4,11},{5,12},{6,13},{7,14},{8,15},{9,16}... | collective-permute-start | bytes 41480 | tf_op jit(solution)/shard_map/ppermute | solution.py:24
  60.0 19.4 %collective-permute-start.3 = (bf16[1,16,3,768]{3,2,1,0:T(4,128)(2,1)S(1)}, bf16[1,16,3,768]{3,2,1,0:T(4,128)(2,1)S(1)}, u32[]{:S(2)}, u32[]{:S(2)}) collective-permute-start(bf16[1,16,3,768]{3,2,1,0:T(4,128)(2,1)S(1)} %get-tuple-element.256), channel_id=1, source_target_pairs={{0,1},{1,2},{2,3},{3,4},{4,5},{5,6},{6,7},{7,8},{8,9},{9,10},{10,1... | collective-permute-start | bytes 221192 | tf_op jit(solution)/shard_map/ppermute | solution.py:24
  62.0 20.0 %collective-permute-start.4 = (bf16[1,16,3,768]{3,2,1,0:T(4,128)(2,1)S(1)}, bf16[1,16,3,768]{3,2,1,0:T(4,128)(2,1)S(1)}, u32[]{:S(2)}, u32[]{:S(2)}) collective-permute-start(bf16[1,16,3,768]{3,2,1,0:T(4,128)(2,1)S(1)} %get-tuple-element.255), channel_id=1, source_target_pairs={{1,0},{2,1},{3,2},{4,3},{5,4},{6,5},{7,6},{8,7},{9,8},{10,9},{11,1... | collective-permute-start | bytes 221192 | tf_op jit(solution)/shard_map/ppermute | solution.py:24
  64.3 37.1 %copy-start.17 = (f32[256]{0:T(256)}, f32[256]{0:T(256)S(1)}, u32[]{:S(2)}) copy-start(f32[256]{0:T(256)S(1)} %get-tuple-element.286) | copy-start | bytes 3076
  65.0 38.7 %copy-start.15 = (f32[256]{0:T(256)}, f32[256]{0:T(256)S(1)}, u32[]{:S(2)}) copy-start(f32[256]{0:T(256)S(1)} %get-tuple-element.284) | copy-start | bytes 3076
  65.7 40.2 %copy-start.13 = (f32[256]{0:T(256)}, f32[256]{0:T(256)S(1)}, u32[]{:S(2)}) copy-start(f32[256]{0:T(256)S(1)} %get-tuple-element.282) | copy-start | bytes 3076
  67.8 44.8 %copy-start.19 = (f32[256]{0:T(256)}, f32[256]{0:T(256)S(1)}, u32[]{:S(2)}) copy-start(f32[256]{0:T(256)S(1)} %get-tuple-element.276) | copy-start | bytes 3076
  68.0 15.8 %collective-permute-start.5 = (bf16[1,3,3,768]{3,2,1,0:T(4,128)(2,1)S(1)}, bf16[1,3,3,768]{3,2,1,0:T(4,128)(2,1)S(1)}, u32[]{:S(2)}, u32[]{:S(2)}) collective-permute-start(bf16[1,3,3,768]{3,2,1,0:T(4,128)(2,1)S(1)} %get-tuple-element.250), channel_id=1, source_target_pairs={{7,0},{8,1},{9,2},{10,3},{11,4},{12,5},{13,6},{14,7},{15,8},{16,9}... | collective-permute-start | bytes 41480 | tf_op jit(solution)/shard_map/ppermute | solution.py:24
  69.6 14.5 %collective-permute-start.6 = (bf16[1,3,16,768]{3,2,1,0:T(8,128)(2,1)S(1)}, bf16[1,3,16,768]{3,2,1,0:T(8,128)(2,1)S(1)}, u32[]{:S(2)}, u32[]{:S(2)}) collective-permute-start(bf16[1,3,16,768]{3,2,1,0:T(8,128)(2,1)S(1)} %get-tuple-element.253), channel_id=1, source_target_pairs={{8,0},{9,1},{10,2},{11,3},{12,4},{13,5},{14,6},{15,7},{16,8},{17,9... | collective-permute-start | bytes 221192 | tf_op jit(solution)/shard_map/ppermute | solution.py:24
  74.6 10.0 %collective-permute-start.7 = (bf16[1,3,3,768]{3,2,1,0:T(4,128)(2,1)S(1)}, bf16[1,3,3,768]{3,2,1,0:T(4,128)(2,1)S(1)}, u32[]{:S(2)}, u32[]{:S(2)}) collective-permute-start(bf16[1,3,3,768]{3,2,1,0:T(4,128)(2,1)S(1)} %get-tuple-element.249), channel_id=1, source_target_pairs={{9,0},{10,1},{11,2},{12,3},{13,4},{14,5},{15,6},{16,7},{17,8},{18,... | collective-permute-start | bytes 41480 | tf_op jit(solution)/shard_map/ppermute | solution.py:24
  115.4 3.9 %copy-start.4 = (f32[256,64]{0,1:T(8,128)S(1)}, f32[256,64]{0,1:T(8,128)}, u32[]{:S(2)}) copy-start(f32[256,64]{0,1:T(8,128)} %get-tuple-element.322) | copy-start | bytes 196612
  115.4 3.9 %copy-start.14 = (f32[256]{0:T(256)S(1)}, f32[256]{0:T(256)}, u32[]{:S(2)}) copy-start(f32[256]{0:T(256)} %copy-done.13) | copy-start | bytes 3076
  115.4 3.9 %copy-start.3 = (f32[256,64]{0,1:T(8,128)S(1)}, f32[256,64]{0,1:T(8,128)}, u32[]{:S(2)}) copy-start(f32[256,64]{0,1:T(8,128)} %get-tuple-element.326) | copy-start | bytes 196612
  115.4 3.9 %copy-start.23 = (f32[256]{0:T(256)S(1)}, f32[256]{0:T(256)}, u32[]{:S(2)}) copy-start(f32[256]{0:T(256)} %get-tuple-element.279) | copy-start | bytes 3076
  115.4 3.9 %copy-start.2 = (f32[256,64]{0,1:T(8,128)S(1)}, f32[256,64]{0,1:T(8,128)}, u32[]{:S(2)}) copy-start(f32[256,64]{0,1:T(8,128)} %get-tuple-element.330) | copy-start | bytes 196612
  115.4 3.9 %copy-start.22 = (f32[256]{0:T(256)S(1)}, f32[256]{0:T(256)}, u32[]{:S(2)}) copy-start(f32[256]{0:T(256)} %get-tuple-element.277) | copy-start | bytes 3076
  115.4 3.9 %copy-start.1 = (f32[256,64]{0,1:T(8,128)S(1)}, f32[256,64]{0,1:T(8,128)}, u32[]{:S(2)}) copy-start(f32[256,64]{0,1:T(8,128)} %get-tuple-element.334) | copy-start | bytes 196612
  115.5 3.9 %copy-start.20 = (f32[256]{0:T(256)S(1)}, f32[256]{0:T(256)}, u32[]{:S(2)}) copy-start(f32[256]{0:T(256)} %copy-done.19) | copy-start | bytes 3076
  115.5 3.9 %copy-start.21 = (f32[256]{0:T(256)S(1)}, f32[256]{0:T(256)}, u32[]{:S(2)}) copy-start(f32[256]{0:T(256)} %get-tuple-element.275) | copy-start | bytes 3076
  117.8 15.0 %collective-permute-start.8 = (bf16[1,3,3,768]{3,2,1,0:T(4,128)(2,1)}, bf16[1,3,3,768]{3,2,1,0:T(4,128)(2,1)}, u32[]{:S(2)}, u32[]{:S(2)}) collective-permute-start(bf16[1,3,3,768]{3,2,1,0:T(4,128)(2,1)} %get-tuple-element.244), channel_id=1, source_target_pairs={{9,0},{10,1},{11,2},{12,3},{13,4},{14,5},{15,6},{16,7},{17,8},{18,... | collective-permute-start | bytes 41480 | tf_op jit(solution)/shard_map/ppermute | solution.py:24
  119.7 32.6 %copy-start.12 = (bf16[1,3,3,768]{3,2,1,0:T(4,128)(2,1)S(1)}, bf16[1,3,3,768]{3,2,1,0:T(4,128)(2,1)}, u32[]{:S(2)}) copy-start(bf16[1,3,3,768]{3,2,1,0:T(4,128)(2,1)} %get-tuple-element.241) | copy-start | bytes 41476
  122.4 21.9 %collective-permute-start.9 = (bf16[1,3,16,768]{3,2,1,0:T(8,128)(2,1)}, bf16[1,3,16,768]{3,2,1,0:T(8,128)(2,1)}, u32[]{:S(2)}, u32[]{:S(2)}) collective-permute-start(bf16[1,3,16,768]{3,2,1,0:T(8,128)(2,1)} %get-tuple-element.246), channel_id=1, source_target_pairs={{8,0},{9,1},{10,2},{11,3},{12,4},{13,5},{14,6},{15,7},{16,8},{17,9... | collective-permute-start | bytes 221192 | tf_op jit(solution)/shard_map/ppermute | solution.py:24
  123.7 28.6 %collective-permute-start.10 = (bf16[1,3,3,768]{3,2,1,0:T(4,128)(2,1)}, bf16[1,3,3,768]{3,2,1,0:T(4,128)(2,1)}, u32[]{:S(2)}, u32[]{:S(2)}) collective-permute-start(bf16[1,3,3,768]{3,2,1,0:T(4,128)(2,1)} %get-tuple-element.243), channel_id=1, source_target_pairs={{7,0},{8,1},{9,2},{10,3},{11,4},{12,5},{13,6},{14,7},{15,8},{16,9}... | collective-permute-start | bytes 41480 | tf_op jit(solution)/shard_map/ppermute | solution.py:24
  125.0 31.4 %collective-permute-start.11 = (bf16[1,16,3,768]{3,2,1,0:T(4,128)(2,1)}, bf16[1,16,3,768]{3,2,1,0:T(4,128)(2,1)}, u32[]{:S(2)}, u32[]{:S(2)}) collective-permute-start(bf16[1,16,3,768]{3,2,1,0:T(4,128)(2,1)} %get-tuple-element.248), channel_id=1, source_target_pairs={{1,0},{2,1},{3,2},{4,3},{5,4},{6,5},{7,6},{8,7},{9,8},{10,9},{11,1... | collective-permute-start | bytes 221192 | tf_op jit(solution)/shard_map/ppermute | solution.py:24
  126.3 33.3 %collective-permute-start.12 = (bf16[1,16,3,768]{3,2,1,0:T(4,128)(2,1)}, bf16[1,16,3,768]{3,2,1,0:T(4,128)(2,1)}, u32[]{:S(2)}, u32[]{:S(2)}) collective-permute-start(bf16[1,16,3,768]{3,2,1,0:T(4,128)(2,1)} %get-tuple-element.247), channel_id=1, source_target_pairs={{0,1},{1,2},{2,3},{3,4},{4,5},{5,6},{6,7},{7,8},{8,9},{9,10},{10,1... | collective-permute-start | bytes 221192 | tf_op jit(solution)/shard_map/ppermute | solution.py:24
  132.8 31.1 %collective-permute-start.13 = (bf16[1,3,3,768]{3,2,1,0:T(4,128)(2,1)}, bf16[1,3,3,768]{3,2,1,0:T(4,128)(2,1)S(1)}, u32[]{:S(2)}, u32[]{:S(2)}) collective-permute-start(bf16[1,3,3,768]{3,2,1,0:T(4,128)(2,1)} %get-tuple-element.242), channel_id=1, source_target_pairs={{0,7},{1,8},{2,9},{3,10},{4,11},{5,12},{6,13},{7,14},{8,15},{9,16}... | collective-permute-start | bytes 41480 | tf_op jit(solution)/shard_map/ppermute | solution.py:24
  144.3 22.9 %collective-permute-start.14 = (bf16[1,3,16,768]{3,2,1,0:T(8,128)(2,1)}, bf16[1,3,16,768]{3,2,1,0:T(8,128)(2,1)S(1)}, u32[]{:S(2)}, u32[]{:S(2)}) collective-permute-start(bf16[1,3,16,768]{3,2,1,0:T(8,128)(2,1)} %get-tuple-element.245), channel_id=1, source_target_pairs={{0,8},{1,9},{2,10},{3,11},{4,12},{5,13},{6,14},{7,15},{8,16},{9,17... | collective-permute-start | bytes 221192 | tf_op jit(solution)/shard_map/ppermute | solution.py:24
  152.3 15.0 %collective-permute-start.15 = (bf16[1,3,3,768]{3,2,1,0:T(4,128)(2,1)S(1)}, bf16[1,3,3,768]{3,2,1,0:T(4,128)(2,1)S(1)}, u32[]{:S(2)}, u32[]{:S(2)}) collective-permute-start(bf16[1,3,3,768]{3,2,1,0:T(4,128)(2,1)S(1)} %copy-done.12), channel_id=1, source_target_pairs={{0,9},{1,10},{2,11},{3,12},{4,13},{5,14},{6,15},{7,16},{8,17},{9,1... | collective-permute-start | bytes 41480 | tf_op jit(solution)/shard_map/ppermute | solution.py:24
  167.9 43.6 %copy-start.7 = (bf16[256,64]{1,0:T(8,128)(2,1)S(1)}, bf16[256,64]{1,0:T(8,128)(2,1)}, u32[]{:S(2)}) copy-start(bf16[256,64]{1,0:T(8,128)(2,1)} %copy.35) | copy-start | bytes 98308
  (19 other events, 52.1 us)
Sparse Core Ops, SparseCore 0:
  10.1 36.0 all-gather.1

commit v2 on v1

v2 whole, which is shorter than its diff:
```python
import jax
import jax.numpy as jnp
from jax import lax
from jax.experimental import pallas as pl
from jax.experimental.pallas import tpu as pltpu
from jax.sharding import PartitionSpec as P

MESH = pl.DeviceIdType.MESH
BF16 = jnp.bfloat16
F32 = jnp.float32
NORM_EPS = 1e-06
NEVER = -1e30
STRIPS = (
    (-1, 0, 0, 48),
    (1, 0, 48, 48),
    (0, -1, 96, 48),
    (0, 1, 144, 48),
    (-1, -1, 192, 16),
    (-1, 1, 208, 16),
    (1, -1, 224, 16),
    (1, 1, 240, 16),
)


def remote(src, dst, send, recv, device):
    return pltpu.make_async_remote_copy(
        src_ref=src,
        dst_ref=dst,
        send_sem=send,
        recv_sem=recv,
        device_id=device,
        device_id_type=MESH,
    )


def dot(a, b):
    return jnp.dot(a, b, preferred_element_type=F32)


def dot_nt(a, b):
    return lax.dot_general(a, b, (((1,), (1,)), ((), ())), preferred_element_type=F32)


def halo_place(j):
    strip = (j >= 48).astype(jnp.int32) + (j >= 96).astype(jnp.int32) + (j >= 144).astype(jnp.int32)
    m = j - 48 * strip
    edge = m >> 4
    along = m & 15
    low = jnp.where((strip & 1) == 0, -3, 16)
    step = jnp.where((strip & 1) == 0, -1, 1)
    level = strip < 2
    row_e = jnp.where(level, low + edge, along)
    col_e = jnp.where(level, along, low + edge)
    rstep_e = jnp.where(level, step, 0)
    cstep_e = jnp.where(level, 0, step)
    k = j - 192
    corner = k >> 4
    n = k & 15
    r3 = n >> 2
    c3 = n & 3
    rstep_c = jnp.where((corner & 2) == 0, -1, 1)
    cstep_c = jnp.where((corner & 1) == 0, -1, 1)
    row_c = jnp.where(rstep_c < 0, -3, 16) + r3
    col_c = jnp.where(cstep_c < 0, -3, 16) + c3
    is_edge = j < 192
    row = jnp.where(is_edge, row_e, row_c)
    col = jnp.where(is_edge, col_e, col_c)
    rstep = jnp.where(is_edge, rstep_e, rstep_c)
    cstep = jnp.where(is_edge, cstep_e, cstep_c)
    filled = is_edge | ((r3 < 3) & (c3 < 3))
    return row, col, rstep, cstep, filled


def owner_token(j):
    row, col, rstep, cstep, filled = halo_place(j)
    return jnp.where(filled, (row - 16 * rstep) * 16 + (col - 16 * cstep), -1)


def kernel(
    tok_ref, w_ref, scale_ref, g_ref, att_ref, gtok_ref, out_ref,
    wp, tok_t, bias, pack, unpack, qkv, inv, qum, gm, kvx, hs, own, ghs, ghr, gq,
    s1, r1, s2, r2, acc, acc_t, s3, r3, acc4, s4, r4, fin,
    wx_send, wx_recv, wc_send, wc_recv, h_send, h_recv, gh_send, gh_recv,
    core_send, core_recv, x_send, x_recv, y_send, y_recv, z_send, z_recv,
):
    img = lax.axis_index("img")
    sp = lax.axis_index("sp")
    x, c = img // 2, img % 2
    y, z = sp // 8, sp % 8
    other_core = (2 * x + 1 - c, sp)
    x_peer = [((2 * ((x + d) % 4) + c), sp) for d in range(4)]
    y_peer = [(img, 8 * ((y + d) % 8) + z) for d in range(8)]
    z_peer = [(img, 8 * y + (z + d) % 8) for d in range(8)]

    def tile_at(rstep, cstep):
        return (img, 8 * ((y + rstep + 8) % 8) + (z + cstep + 8) % 8)

    barrier = pltpu.get_barrier_semaphore()
    peers = [other_core] + x_peer[1:] + y_peer[1:] + z_peer[1:]
    peers += [tile_at(r, s) for r in (-1, 1) for s in (-1, 1)]
    for peer in peers:
        pl.semaphore_signal(barrier, inc=1, device_id=peer, device_id_type=MESH)

    def block(b):
        return pl.ds(pl.multiple_of(96 * b, 32), 96)

    for p in range(3):
        for part in range(3):
            low = 384 * part + 128 * p
            wp[p, block(img), 128 * part : 128 * part + 128] = w_ref[:, low : low + 128]
    pl.semaphore_wait(barrier, len(peers))

    wx, wc = {}, {}
    for p in range(3):
        mine = wp.at[p, block(img)]
        wc[p, 0] = remote(mine, mine, wc_send.at[p, 0], wc_recv.at[p, 0], other_core)
        wc[p, 0].start()
        for d in (1, 3, 2):
            wx[p, d] = remote(mine, mine, wx_send.at[p, d - 1], wx_recv.at[p, d - 1], x_peer[d])
            wx[p, d].start()

    def forward_weights(p):
        for d in (1, 3, 2):
            wx[p, d].wait_recv()
            got = wp.at[p, block(2 * ((x + 4 - d) % 4) + c)]
            wc[p, d] = remote(got, got, wc_send.at[p, d], wc_recv.at[p, d], other_core)
            wc[p, d].start()

    for b in range(8):
        tok_t[b] = tok_ref[:, 96 * b : 96 * b + 96].astype(F32).T.astype(BF16)
    query = lax.broadcasted_iota(jnp.int32, (1, 256), 1)
    query_row, query_col = query >> 4, query & 15

    def put_bias(low, key_row, key_col):
        near = (jnp.abs(key_row - query_row) <= 3) & (jnp.abs(key_col - query_col) <= 3)
        bias[low : low + 256] = jnp.where(near, 0.0, NEVER).astype(F32)

    j_rows = lax.broadcasted_iota(jnp.int32, (256, 1), 0)
    put_bias(0, j_rows >> 4, j_rows & 15)
    row, col, _, _, filled = halo_place(j_rows)
    grow, gcol = row + 16 * y, col + 16 * z
    inside = filled & (grow >= 0) & (grow < 128) & (gcol >= 0) & (gcol < 128)
    put_bias(256, jnp.where(inside, row, 1000), col)
    j_cols = lax.broadcasted_iota(jnp.int32, (1, 256), 1)
    wide_rows = lax.broadcasted_iota(jnp.int32, (256, 256), 0)
    wide_cols = lax.broadcasted_iota(jnp.int32, (256, 256), 1)
    pack[...] = jnp.where(owner_token(j_rows) == wide_cols, 1.0, 0.0).astype(BF16)
    unpack[...] = jnp.where(owner_token(j_cols) == wide_rows, 1.0, 0.0).astype(BF16)
    lane_r = lax.broadcasted_iota(jnp.int32, (128, 128), 0)
    lane_c = lax.broadcasted_iota(jnp.int32, (128, 128), 1)
    same_head = jnp.where((lane_r >> 6) == (lane_c >> 6), 1.0, 0.0).astype(BF16)
    eye = jnp.where(lane_r == lane_c, 1.0, 0.0).astype(BF16)
    lane = lax.broadcasted_iota(jnp.int32, (1, 128), 1)
    head_mask = [jnp.where((lane >> 6) == e, 1.0, 0.0).astype(F32) for e in range(2)]
    for p in range(3):
        g_pair = g_ref[:, 128 * p : 128 * p + 128].astype(F32)
        for e in range(2):
            gm[p, e] = (g_pair * head_mask[e]).astype(BF16)

    def head_sum(v):
        high = v.astype(BF16)
        low = (v - high.astype(F32)).astype(BF16)
        return dot(high, same_head) + dot(low, same_head)

    halo, back = {}, {}

    def project(p):
        for d in range(4):
            wc[p, d].wait_recv()
        low = dot(tok_ref[...], wp[p]).astype(BF16)
        qkv[p] = low
        q = low[:, 0:128].astype(F32)
        k = low[:, 128:256].astype(F32)
        inv_q = lax.rsqrt(head_sum(q * q) * (1.0 / 64.0) + NORM_EPS) * 0.125
        inv_k = lax.rsqrt(head_sum(k * k) * (1.0 / 64.0) + NORM_EPS) * 0.125
        inv[p, :, 0:128] = inv_q
        inv[p, :, 128:256] = inv_k
        q_unit = q * inv_q
        for e in range(2):
            qum[p, e] = (q_unit * head_mask[e]).astype(BF16)
        kvx[p, 0:256, 0:128] = (k * inv_k).astype(BF16)
        kvx[p, 0:256, 128:256] = low[:, 256:384]
        hs[p] = dot(pack[...], kvx[p, 0:256]).astype(BF16)
        for s, (rstep, cstep, first, rows) in enumerate(STRIPS):
            halo[p, s] = remote(
                hs.at[p, pl.ds(first, rows)],
                kvx.at[p, pl.ds(256 + first, rows)],
                h_send.at[p, s],
                h_recv.at[p, s],
                tile_at(-rstep, -cstep),
            )
            halo[p, s].start()

    def attend(p):
        for s in range(8):
            halo[p, s].wait_recv()
        key = kvx[p, :, 0:128]
        value = kvx[p, :, 128:256]
        key_t = dot_nt(eye, key).astype(BF16)
        value_t = dot_nt(eye, value).astype(BF16)
        att_t, gq_t = [], []
        grad_k, grad_v = None, None
        for e in range(2):
            scale = scale_ref[2 * p + e]
            rows = slice(64 * e, 64 * e + 64)
            raised = jnp.exp(dot_nt(key, qum[p, e]) * scale + bias[...])
            attention = raised * (1.0 / jnp.sum(raised, axis=0, keepdims=True))
            att_low = attention.astype(BF16)
            grad_att = dot_nt(value, gm[p, e])
            row_total = jnp.sum(attention * grad_att, axis=0, keepdims=True)
            grad_s = (attention * scale * (grad_att - row_total)).astype(BF16)
            att_t.append(dot(value_t[rows], att_low))
            gq_t.append(dot(key_t[rows], grad_s))
            grad_v_e = dot(att_low, gm[p, e])
            grad_k_e = dot(grad_s, qum[p, e])
            grad_v = grad_v_e if grad_v is None else grad_v + grad_v_e
            grad_k = grad_k_e if grad_k is None else grad_k + grad_k_e
        ghs[p, :, 0:128] = grad_k[256:512].astype(BF16)
        ghs[p, :, 128:256] = grad_v[256:512].astype(BF16)
        for s, (rstep, cstep, first, rows) in enumerate(STRIPS):
            span = pl.ds(first, rows)
            back[p, s] = remote(
                ghs.at[p, span], ghr.at[p, span], gh_send.at[p, s], gh_recv.at[p, s], tile_at(rstep, cstep)
            )
            back[p, s].start()
        own[p, :, 0:128] = grad_k[0:256]
        own[p, :, 128:256] = grad_v[0:256]
        att_ref[:, 128 * p : 128 * p + 128] = jnp.concatenate(att_t, axis=0).T.astype(BF16)
        grad_q = jnp.concatenate(gq_t, axis=0).T
        q = qkv[p, :, 0:128].astype(F32)
        inv_q = inv[p, :, 0:128]
        gq[p, :, 0:128] = (inv_q * (grad_q - q * (inv_q * inv_q) * head_sum(grad_q * q))).astype(BF16)

    def product(p, b):
        return dot(tok_t[b], gq[p])

    core, cross = {}, {}

    def finish(p):
        for s in range(8):
            back[p, s].wait_recv()
        grad_kv = own[p] + dot(unpack[...], ghr[p])
        grad_k = grad_kv[:, 0:128]
        k = qkv[p, :, 128:256].astype(F32)
        inv_k = inv[p, :, 128:256]
        gq[p, :, 128:256] = (inv_k * (grad_k - k * (inv_k * inv_k) * head_sum(grad_k * k))).astype(BF16)
        gq[p, :, 256:384] = grad_kv[:, 128:256].astype(BF16)
        for n in range(4):
            s1[p, n] = product(p, 2 * n + 1 - c).astype(BF16)
        core[p] = remote(s1.at[p], r1.at[p], core_send.at[p], core_recv.at[p], other_core)
        core[p].start()

    def cross_send(p):
        core[p].wait_recv()
        for d in (1, 3, 2):
            to = (x + d) % 4
            s2[p, d - 1] = (product(p, 2 * to + c) + r1[p, to].astype(F32)).astype(BF16)
            cross[p, d] = remote(
                s2.at[p, d - 1], r2.at[p, d - 1], x_send.at[p, d - 1], x_recv.at[p, d - 1], x_peer[d]
            )
            cross[p, d].start()
        acc[p, 0:96] = product(p, img) + r1[p, x].astype(F32)

    def cross_sum(p):
        total = acc[p, 0:96]
        for d in (1, 3, 2):
            cross[p, d].wait_recv()
            total += r2[p, d - 1].astype(F32)
        acc[p, 0:96] = total
        turned = acc[p].T
        for part in range(3):
            low = 384 * part + 128 * p
            acc_t[low : low + 128] = turned[128 * part : 128 * part + 128]

    forward_weights(0)
    project(0)
    forward_weights(1)
    project(1)
    forward_weights(2)
    attend(0)
    project(2)
    attend(1)
    finish(0)
    acc[:, 96:128, :] = jnp.zeros((3, 32, 384), F32)
    acc4[...] = jnp.zeros_like(acc4)
    fin[...] = jnp.zeros_like(fin)
    attend(2)
    finish(1)
    cross_send(0)
    finish(2)
    cross_send(1)
    cross_send(2)
    grad_tokens = dot_nt(gq[0], wp[0]) + dot_nt(gq[1], wp[1]) + dot_nt(gq[2], wp[2])
    gtok_ref[...] = grad_tokens.astype(BF16)
    for p in range(3):
        cross_sum(p)

    y_copies = []
    for d in range(1, 8):
        to = (y + d) % 8
        s3[d - 1] = acc_t[pl.ds(pl.multiple_of(144 * to, 16), 144)].astype(BF16)
        copy = remote(s3.at[d - 1], r3.at[d - 1], y_send.at[d - 1], y_recv.at[d - 1], y_peer[d])
        copy.start()
        y_copies.append(copy)
    total = acc_t[pl.ds(pl.multiple_of(144 * y, 16), 144)]
    for d in range(7):
        y_copies[d].wait_recv()
        total += r3[d].astype(F32)
    acc4[0:144] = total
    for n in range(8):
        s4[n] = acc4[18 * n : 18 * n + 24]
    z_copies = []
    for d in range(1, 8):
        copy = remote(
            s4.at[(z + d) % 8], r4.at[d - 1], z_send.at[d - 1], z_recv.at[d - 1], z_peer[d]
        )
        copy.start()
        z_copies.append(copy)
    total = s4[z]
    for d in range(7):
        z_copies[d].wait_recv()
        total += r4[d]
    fin[0:24] = total * (1.0 / 8.0)
    out_ref[...] = fin[...].T[0:96, 0:18]

    started = list(wx.values()) + list(wc.values()) + list(halo.values()) + list(back.values())
    started += list(core.values()) + list(cross.values()) + y_copies + z_copies
    for copy in started:
        copy.wait_send()


def local(tokens, w_qkv, score_scale, grad_out):
    dma = pltpu.SemaphoreType.DMA
    vmem = pl.BlockSpec(memory_space=pltpu.VMEM)
    attended, grad_tokens, weight_grad = pl.pallas_call(
        kernel,
        out_shape=(
            jax.ShapeDtypeStruct((256, 384), BF16),
            jax.ShapeDtypeStruct((256, 768), BF16),
            jax.ShapeDtypeStruct((96, 18), F32),
        ),
        in_specs=[vmem, vmem, pl.BlockSpec(memory_space=pltpu.SMEM), vmem],
        out_specs=(vmem, vmem, vmem),
        scratch_shapes=[
            pltpu.VMEM((3, 768, 384), BF16),
            pltpu.VMEM((8, 96, 256), BF16),
            pltpu.VMEM((512, 256), F32),
            pltpu.VMEM((256, 256), BF16),
            pltpu.VMEM((256, 256), BF16),
            pltpu.VMEM((3, 256, 384), BF16),
            pltpu.VMEM((3, 256, 256), F32),
            pltpu.VMEM((3, 2, 256, 128), BF16),
            pltpu.VMEM((3, 2, 256, 128), BF16),
            pltpu.VMEM((3, 512, 256), BF16),
            pltpu.VMEM((3, 256, 256), BF16),
            pltpu.VMEM((3, 256, 256), F32),
            pltpu.VMEM((3, 256, 256), BF16),
            pltpu.VMEM((3, 256, 256), BF16),
            pltpu.VMEM((3, 256, 384), BF16),
            pltpu.VMEM((3, 4, 96, 384), BF16),
            pltpu.VMEM((3, 4, 96, 384), BF16),
            pltpu.VMEM((3, 3, 96, 384), BF16),
            pltpu.VMEM((3, 3, 96, 384), BF16),
            pltpu.VMEM((3, 128, 384), F32),
            pltpu.VMEM((1152, 128), F32),
            pltpu.VMEM((7, 144, 128), BF16),
            pltpu.VMEM((7, 144, 128), BF16),
            pltpu.VMEM((152, 128), F32),
            pltpu.VMEM((8, 24, 128), F32),
            pltpu.VMEM((7, 24, 128), F32),
            pltpu.VMEM((128, 128), F32),
            dma((3, 3)), dma((3, 3)), dma((3, 4)), dma((3, 4)),
            dma((3, 8)), dma((3, 8)), dma((3, 8)), dma((3, 8)),
            dma((3,)), dma((3,)), dma((3, 3)), dma((3, 3)),
            dma((7,)), dma((7,)), dma((7,)), dma((7,)),
        ],
        compiler_params=pltpu.CompilerParams(
            collective_id=0, has_side_effects=True, vmem_limit_bytes=40 * 1024 * 1024
        ),
    )(tokens.reshape(256, 768), w_qkv, score_scale, grad_out.reshape(256, 384))
    return (
        attended.reshape(1, 1, 16, 16, 384),
        grad_tokens.reshape(1, 1, 16, 16, 768),
        weight_grad,
    )


def solution(mesh):
    return jax.shard_map(
        local,
        mesh=mesh,
        in_specs=(
            P("img", "sp", None, None, None),
            P("img", None),
            P(),
            P("img", "sp", None, None, None),
        ),
        out_specs=(
            P("img", "sp", None, None, None),
            P("img", "sp", None, None, None),
            P("img", "sp"),
        ),
        check_vma=False,
    )
```

time: 224 us -> 71.4 us (0.32)
  starting transfers between devices: 50 us -> 0 us
  waiting for transfers between devices: 31.4 us -> 0 us
  matrix products: 29.7 us -> 0 us
  local copies, waits for them, and re-layouts: 30.1 us -> 5.61 us
  other arithmetic: 23 us -> 0 us
  Pallas kernels: 41.9 us -> 64.7 us
  between operations: 15.5 us -> 0.65 us
    ppermute x16 -> x0, starting transfers between devices: 49.9 us -> none  [passed_along(): return lax.ppermute(x, axis, pairs)]
    all_gather x1 -> x0, waiting for transfers between devices: 30.7 us -> none  [local(): full_weights = lax.all_gather(w_qkv, 'img', axis=0, tiled=True)]
    dot_general x38 -> x0, matrix products: 29.7 us -> none  [the longest x6 8.1 us: block_pass(): jnp.dot(grad_scores, key_unit, preferred_element_type=jnp.float32)]
    pallas_call x1, Pallas kernels: 41.9 us -> 64.7 us  [local(): pl.pallas_call(kernel, out_shape=(jax.ShapeDtypeStruct((256, 384), BF16),...]
    another operation x11 -> x0, other arithmetic: 10 us -> none
    scatter x9 -> x0, local copies, waits for them, and re-layouts: 8.8 us -> none  [the longest x8 8.66 us: local(): extended.at[:, erow_low:erow_high, ecol_low:ecol_high].set(arrived)]
    scatter-add x6 -> x0, local copies, waits for them, and re-layouts: 7.85 us -> none  [local(): owned = owned.at[:, row_low:row_high, col_low:col_high].add(arrived)]
    another operation x17 -> x0, local copies, waits for them, and re-layouts: 4.9 us -> none
  transfers between devices with their start and end apart: 17 -> 0, of which waited for: 1 -> 0; matrix products, arithmetic and copies ran while one was open for 19% -> 0% of each run, Pallas kernels for 0% -> 0%
where the time goes in v2:
time: 71.4 us; the launch traced here: 71 us
  Pallas kernels  64.7 us (91%)
  local copies, waits for them, and re-layouts  5.61 us (8%)
    pallas_call x1, Pallas kernels, local(): pl.pallas_call(kernel, out_shape=(jax.ShapeDtypeStruct((256, 384), BF16),...  64.7 us
    unnamed x11, local copies, waits for them, and re-layouts  5.61 us

profile of v2, /device:TPU:1, one launch (start us, length us, event | category | flops | bytes accessed | tf_op | source)
XLA Modules:
  0.0 71.0 jit_solution(11395165020458950655)
XLA Ops:
  0.6 0.0 copy-start.3
  0.6 0.6 copy-done.3
  1.3 0.0 copy-start
  1.3 1.0 %copy-done = bf16[1,1,16,16,768]{4,3,2,1,0:T(8,128)(2,1)S(1)} copy-done((bf16[1,1,16,16,768]{4,3,2,1,0:T(8,128)(2,1)S(1)}, bf16[1,1,16,16,768]{4,3,2,1,0:T(8,128)(2,1)}, u32[]{:S(2)}) %copy-start) | copy-done | bytes 393240
  2.3 0.0 copy-start.1
  2.3 0.9 %copy-done.1 = bf16[96,1152]{1,0:T(8,128)(2,1)S(1)} copy-done((bf16[96,1152]{1,0:T(8,128)(2,1)S(1)}, bf16[96,1152]{1,0:T(8,128)(2,1)}, u32[]{:S(2)}) %copy-start.1) | copy-done | bytes 221208
  3.2 0.0 copy-start.2
  3.2 0.9 %copy-done.2 = bf16[1,1,16,16,384]{4,3,2,1,0:T(8,128)(2,1)S(1)} copy-done((bf16[1,1,16,16,384]{4,3,2,1,0:T(8,128)(2,1)S(1)}, bf16[1,1,16,16,384]{4,3,2,1,0:T(8,128)(2,1)}, u32[]{:S(2)}) %copy-start.2) | copy-done | bytes 196632
  4.1 64.7 %shard_map.67 = (bf16[256,384]{1,0:T(8,128)(2,1)S(1)}, bf16[256,768]{1,0:T(8,128)(2,1)S(1)}, f32[96,18]{1,0:T(8,128)S(1)}) custom-call(bf16[256,768]{1,0:T(8,128)(2,1)S(1)} %bitcast.5, bf16[96,1152]{1,0:T(8,128)(2,1)S(1)} %copy-done.1, f32[6]{0:T(128)S(1)} %copy-done.3, bf16[256,384]{1,0:T(8,128)(2,1)S(1)} %bitcast.7), custom_call_target="tpu_custom_call" | custom-call | tf_op jit(solution)/shard_map/pallas_call | solution.py:335
  68.9 0.7 copy.7
  69.6 0.7 copy.10
  70.2 0.7 %copy.11 = bf16[1,1,16,16,768]{4,3,2,1,0:T(8,128)(2,1)} copy(bf16[1,1,16,16,768]{4,3,2,1,0:T(8,128)(2,1)S(1)} %bitcast.4) | data formatting | bytes 786432
Async XLA Ops:
  0.6 0.7 copy-start.3
  1.3 1.0 %copy-start = (bf16[1,1,16,16,768]{4,3,2,1,0:T(8,128)(2,1)S(1)}, bf16[1,1,16,16,768]{4,3,2,1,0:T(8,128)(2,1)}, u32[]{:S(2)}) copy-start(bf16[1,1,16,16,768]{4,3,2,1,0:T(8,128)(2,1)} %param.4) | copy-start | bytes 1179652
  2.3 0.9 %copy-start.1 = (bf16[96,1152]{1,0:T(8,128)(2,1)S(1)}, bf16[96,1152]{1,0:T(8,128)(2,1)}, u32[]{:S(2)}) copy-start(bf16[96,1152]{1,0:T(8,128)(2,1)} %w_ref.1) | copy-start | bytes 663556
  3.2 0.9 %copy-start.2 = (bf16[1,1,16,16,384]{4,3,2,1,0:T(8,128)(2,1)S(1)}, bf16[1,1,16,16,384]{4,3,2,1,0:T(8,128)(2,1)}, u32[]{:S(2)}) copy-start(bf16[1,1,16,16,384]{4,3,2,1,0:T(8,128)(2,1)} %param.7) | copy-start | bytes 589828

commit v3 on v2

v3 whole, which is shorter than its diff:
```python
import jax
import jax.numpy as jnp
from jax import lax
from jax.experimental import pallas as pl
from jax.experimental.pallas import tpu as pltpu
from jax.sharding import PartitionSpec as P

MESH = pl.DeviceIdType.MESH
BF16 = jnp.bfloat16
F32 = jnp.float32
NORM_EPS = 1e-06
NEVER = -1e30
STRIPS = (
    (-1, 0, 0, 48),
    (1, 0, 48, 48),
    (0, -1, 96, 48),
    (0, 1, 144, 48),
    (-1, -1, 192, 16),
    (-1, 1, 208, 16),
    (1, -1, 224, 16),
    (1, 1, 240, 16),
)


def remote(src, dst, send, recv, device):
    return pltpu.make_async_remote_copy(
        src_ref=src,
        dst_ref=dst,
        send_sem=send,
        recv_sem=recv,
        device_id=device,
        device_id_type=MESH,
    )


def dot(a, b):
    return jnp.dot(a, b, preferred_element_type=F32)


def dot_nt(a, b):
    return lax.dot_general(a, b, (((1,), (1,)), ((), ())), preferred_element_type=F32)


def halo_place(j):
    strip = (j >= 48).astype(jnp.int32) + (j >= 96).astype(jnp.int32) + (j >= 144).astype(jnp.int32)
    m = j - 48 * strip
    edge = m >> 4
    along = m & 15
    low = jnp.where((strip & 1) == 0, -3, 16)
    step = jnp.where((strip & 1) == 0, -1, 1)
    level = strip < 2
    row_e = jnp.where(level, low + edge, along)
    col_e = jnp.where(level, along, low + edge)
    rstep_e = jnp.where(level, step, 0)
    cstep_e = jnp.where(level, 0, step)
    k = j - 192
    corner = k >> 4
    n = k & 15
    r3 = n >> 2
    c3 = n & 3
    rstep_c = jnp.where((corner & 2) == 0, -1, 1)
    cstep_c = jnp.where((corner & 1) == 0, -1, 1)
    row_c = jnp.where(rstep_c < 0, -3, 16) + r3
    col_c = jnp.where(cstep_c < 0, -3, 16) + c3
    is_edge = j < 192
    row = jnp.where(is_edge, row_e, row_c)
    col = jnp.where(is_edge, col_e, col_c)
    rstep = jnp.where(is_edge, rstep_e, rstep_c)
    cstep = jnp.where(is_edge, cstep_e, cstep_c)
    filled = is_edge | ((r3 < 3) & (c3 < 3))
    return row, col, rstep, cstep, filled


def owner_token(j):
    row, col, rstep, cstep, filled = halo_place(j)
    return jnp.where(filled, (row - 16 * rstep) * 16 + (col - 16 * cstep), -1)


def kernel(
    tok_hbm, w_hbm, scale_hbm, g_hbm, att_hbm, gtok_hbm, out_ref,
    tokx, g_ref, scale_ref, att_ref, gtok_ref, wp, tok_t, tok_2, bias, pack, unpack, qk, inv, qum, gm, kvx, hs, own,
    ghs, ghr, gq, s2, r2, acc, acc_t, ya, zb, sya, szb, rya, rzb, ta, tb, sza, rza, ryb, fin,
    in_sem, w_sem, out_sem, wx_send, wx_recv, wc_send, wc_recv, h_send, h_recv, gh_send, gh_recv,
    tok_send, tok_recv, core_send, core_recv, x_send, x_recv, ya_send, ya_recv, zb_send, zb_recv,
    za_send, za_recv, yb_send, yb_recv,
):
    img = lax.axis_index("img")
    sp = lax.axis_index("sp")
    x, c = img // 2, img % 2
    y, z = sp // 8, sp % 8
    other_core = (2 * x + 1 - c, sp)
    x_peer = [((2 * ((x + d) % 4) + c), sp) for d in range(4)]
    y_peer = [(img, 8 * ((y + d) % 8) + z) for d in range(8)]
    z_peer = [(img, 8 * y + (z + d) % 8) for d in range(8)]

    def tile_at(rstep, cstep):
        return (img, 8 * ((y + rstep + 8) % 8) + (z + cstep + 8) % 8)

    barrier = pltpu.get_barrier_semaphore()
    peers = [other_core] + x_peer[1:] + y_peer[1:] + z_peer[1:]
    peers += [tile_at(r, s) for r in (-1, 1) for s in (-1, 1)]
    for peer in peers:
        pl.semaphore_signal(barrier, inc=1, device_id=peer, device_id_type=MESH)

    def block(b):
        return pl.ds(pl.multiple_of(96 * b, 32), 96)

    loads = [
        pltpu.make_async_copy(tok_hbm, tokx.at[pl.ds(0, 256)], in_sem.at[0]),
        pltpu.make_async_copy(g_hbm, g_ref, in_sem.at[1]),
        pltpu.make_async_copy(scale_hbm, scale_ref, in_sem.at[2]),
    ]
    w_loads = [
        pltpu.make_async_copy(
            w_hbm.at[:, pl.ds(384 * part + 128 * p, 128)],
            wp.at[p, block(img), pl.ds(128 * part, 128)],
            w_sem.at[p, part],
        )
        for p in range(3)
        for part in range(3)
    ]
    for load in w_loads + loads:
        load.start()
    query = lax.broadcasted_iota(jnp.int32, (1, 256), 1)
    query_row, query_col = query >> 4, query & 15

    def put_bias(low, key_row, key_col):
        near = (jnp.abs(key_row - query_row) <= 3) & (jnp.abs(key_col - query_col) <= 3)
        bias[low : low + 256] = jnp.where(near, 0.0, NEVER).astype(F32)

    j_rows = lax.broadcasted_iota(jnp.int32, (256, 1), 0)
    put_bias(0, j_rows >> 4, j_rows & 15)
    row, col, _, _, filled = halo_place(j_rows)
    grow, gcol = row + 16 * y, col + 16 * z
    inside = filled & (grow >= 0) & (grow < 128) & (gcol >= 0) & (gcol < 128)
    put_bias(256, jnp.where(inside, row, 1000), col)
    j_cols = lax.broadcasted_iota(jnp.int32, (1, 256), 1)
    wide_rows = lax.broadcasted_iota(jnp.int32, (256, 256), 0)
    wide_cols = lax.broadcasted_iota(jnp.int32, (256, 256), 1)
    pack[...] = jnp.where(owner_token(j_rows) == wide_cols, 1.0, 0.0).astype(BF16)
    unpack[...] = jnp.where(owner_token(j_cols) == wide_rows, 1.0, 0.0).astype(BF16)
    lane_r = lax.broadcasted_iota(jnp.int32, (128, 128), 0)
    lane_c = lax.broadcasted_iota(jnp.int32, (128, 128), 1)
    same_head = jnp.where((lane_r >> 6) == (lane_c >> 6), 1.0, 0.0).astype(BF16)
    eye = jnp.where(lane_r == lane_c, 1.0, 0.0).astype(BF16)
    lane = lax.broadcasted_iota(jnp.int32, (1, 128), 1)
    head_mask = [jnp.where((lane >> 6) == e, 1.0, 0.0).astype(F32) for e in range(2)]

    for load in w_loads:
        load.wait()
    pl.semaphore_wait(barrier, len(peers))

    wx, wc = {}, {}

    def to_core(p, n, ref):
        wc[p, n] = remote(ref, ref, wc_send.at[p, n], wc_recv.at[p, n], other_core)
        wc[p, n].start()

    def to_x(p, n, ref, d):
        wx[p, n] = remote(ref, ref, wx_send.at[p, n], wx_recv.at[p, n], x_peer[d])
        wx[p, n].start()

    def half(b, h):
        return pl.ds(pl.multiple_of(96 * b + 48 * h, 16), 48)

    left, right, across = [2 * ((x + d) % 4) + c for d in (3, 1, 2)]
    for p in range(3):
        mine = wp.at[p, block(img)]
        to_x(p, 0, mine, 1)
        to_x(p, 1, mine, 3)
        to_core(p, 0, mine)

    for load in loads:
        load.wait()
    hs[...] = dot(pack[...], tokx[0:256]).astype(BF16)
    halo = {}
    for s, (rstep, cstep, first, rows) in reversed(list(enumerate(STRIPS))):
        halo[s] = remote(
            hs.at[pl.ds(first, rows)],
            tokx.at[pl.ds(256 + first, rows)],
            h_send.at[s],
            h_recv.at[s],
            tile_at(-rstep, -cstep),
        )
        halo[s].start()

    def pass_on(p):
        wx[p, 0].wait_recv()
        to_x(p, 2, wp.at[p, half(left, 0)], 1)
        to_core(p, 1, wp.at[p, block(left)])
        wx[p, 1].wait_recv()
        to_x(p, 3, wp.at[p, half(right, 1)], 3)
        to_core(p, 2, wp.at[p, block(right)])

    def pass_core(p):
        for h in range(2):
            wx[p, 2 + h].wait_recv()
            to_core(p, 3 + h, wp.at[p, half(across, h)])

    for p in range(3):
        g_pair = g_ref[:, 128 * p : 128 * p + 128].astype(F32)
        for e in range(2):
            gm[p, e] = (g_pair * head_mask[e]).astype(BF16)

    for b in range(8):
        tok_t[b // 2, b % 2] = tokx[0:256, 96 * b : 96 * b + 96].astype(F32).T.astype(BF16)
    tokens_out = remote(
        tok_t.at[:, 1 - c], tok_2.at[:, :, pl.ds(256, 256)], tok_send, tok_recv, other_core
    )
    tokens_out.start()
    tok_2[:, :, 0:256] = tok_t[:, c]

    def head_sum(v):
        high = v.astype(BF16)
        low = (v - high.astype(F32)).astype(BF16)
        return dot(high, same_head) + dot(low, same_head)

    back, core, cross = {}, {}, {}

    def exchange(p, n, lanes):
        core[p, n] = remote(
            gq.at[p, pl.ds(0, 256), lanes],
            gq.at[p, pl.ds(256, 256), lanes],
            core_send.at[p, n],
            core_recv.at[p, n],
            other_core,
        )
        core[p, n].start()

    def project(p):
        for n in range(5):
            wc[p, n].wait_recv()
        low = dot(tokx[0:256], wp[p]).astype(BF16)
        far = dot(tokx[256:512], wp[p, :, 128:384]).astype(BF16)
        qk[p] = low[:, 0:256]
        q = low[:, 0:128].astype(F32)
        k = low[:, 128:256].astype(F32)
        k_far = far[:, 0:128].astype(F32)
        inv_q = lax.rsqrt(head_sum(q * q) * (1.0 / 64.0) + NORM_EPS) * 0.125
        inv_k = lax.rsqrt(head_sum(k * k) * (1.0 / 64.0) + NORM_EPS) * 0.125
        inv_far = lax.rsqrt(head_sum(k_far * k_far) * (1.0 / 64.0) + NORM_EPS) * 0.125
        inv[p, :, 0:128] = inv_q
        inv[p, :, 128:256] = inv_k
        q_unit = q * inv_q
        for e in range(2):
            qum[p, e] = (q_unit * head_mask[e]).astype(BF16)
        kvx[p, 0:256, 0:128] = (k * inv_k).astype(BF16)
        kvx[p, 0:256, 128:256] = low[:, 256:384]
        kvx[p, 256:512, 0:128] = (k_far * inv_far).astype(BF16)
        kvx[p, 256:512, 128:256] = far[:, 128:256]

    def attend(p):
        key = kvx[p, :, 0:128]
        value = kvx[p, :, 128:256]
        key_t = dot_nt(eye, key).astype(BF16)
        value_t = dot_nt(eye, value).astype(BF16)
        att_t, gq_t = [], []
        grad_k, grad_v = None, None
        for e in range(2):
            scale = scale_ref[2 * p + e]
            rows = slice(64 * e, 64 * e + 64)
            raised = jnp.exp(dot_nt(key, qum[p, e]) * scale + bias[...])
            attention = raised * (1.0 / jnp.sum(raised, axis=0, keepdims=True))
            att_low = attention.astype(BF16)
            grad_att = dot_nt(value, gm[p, e])
            row_total = jnp.sum(attention * grad_att, axis=0, keepdims=True)
            grad_s = (attention * scale * (grad_att - row_total)).astype(BF16)
            att_t.append(dot(value_t[rows], att_low))
            gq_t.append(dot(key_t[rows], grad_s))
            grad_v_e = dot(att_low, gm[p, e])
            grad_k_e = dot(grad_s, qum[p, e])
            grad_v = grad_v_e if grad_v is None else grad_v + grad_v_e
            grad_k = grad_k_e if grad_k is None else grad_k + grad_k_e
        ghs[p, :, 0:128] = grad_k[256:512].astype(BF16)
        ghs[p, :, 128:256] = grad_v[256:512].astype(BF16)
        for s, (rstep, cstep, first, rows) in enumerate(STRIPS):
            span = pl.ds(first, rows)
            back[p, s] = remote(
                ghs.at[p, span], ghr.at[p, span], gh_send.at[p, s], gh_recv.at[p, s], tile_at(rstep, cstep)
            )
            back[p, s].start()
        own[p, :, 0:128] = grad_k[0:256]
        own[p, :, 128:256] = grad_v[0:256]
        att_ref[:, 128 * p : 128 * p + 128] = jnp.concatenate(att_t, axis=0).T.astype(BF16)
        grad_q = jnp.concatenate(gq_t, axis=0).T
        q = qk[p, :, 0:128].astype(F32)
        inv_q = inv[p, :, 0:128]
        gq[p, 0:256, 0:128] = (inv_q * (grad_q - q * (inv_q * inv_q) * head_sum(grad_q * q))).astype(BF16)
        exchange(p, 0, pl.ds(0, 128))

    def finish(p):
        for s in range(8):
            back[p, s].wait_recv()
        grad_kv = own[p] + dot(unpack[...], ghr[p])
        grad_k = grad_kv[:, 0:128]
        k = qk[p, :, 128:256].astype(F32)
        inv_k = inv[p, :, 128:256]
        gq[p, 0:256, 128:256] = (inv_k * (grad_k - k * (inv_k * inv_k) * head_sum(grad_k * k))).astype(BF16)
        gq[p, 0:256, 256:384] = grad_kv[:, 128:256].astype(BF16)
        exchange(p, 1, pl.ds(128, 256))

    def cross_send(p, part):
        core[p, part].wait_recv()
        lanes = slice(128, 384) if part else slice(0, 128)
        span = pl.ds(128, 256) if part else pl.ds(0, 128)
        mine = gq[p, :, lanes]
        for d in (2, 1, 3):
            s2[p, d - 1, :, lanes] = dot(tok_2[(x + d) % 4], mine).astype(BF16)
            cross[p, part, d] = remote(
                s2.at[p, d - 1, :, span],
                r2.at[p, d - 1, :, span],
                x_send.at[p, part, d - 1],
                x_recv.at[p, part, d - 1],
                x_peer[d],
            )
            cross[p, part, d].start()
        acc[p, 0:96, lanes] = dot(tok_2[x], mine)

    stages = [(0, 0), (1, 0), (0, 1), (2, 0), (1, 1), (2, 1)]

    def stage_of(n):
        return stages.index((n % 384 // 128, min(n // 384, 1)))

    def cross_sum(p, part):
        lanes = slice(128, 384) if part else slice(0, 128)
        for d in (1, 3, 2):
            cross[p, part, d].wait_recv()
        total = acc[p, 0:96, lanes]
        for d in range(3):
            total += r2[p, d, :, lanes].astype(F32)
        acc[p, 0:96, lanes] = total
        for n in (1, 2) if part else (0,):
            low = 384 * n + 128 * p
            acc_t[low : low + 128] = acc[p, :, 128 * n : 128 * n + 128].T
        for s in range(64):
            if max(stage_of(18 * s + i) for i in range(18)) == stages.index((p, part)):
                ya[s // 8, 10 * (s % 8) : 10 * (s % 8) + 10] = acc_t[18 * s : 18 * s + 10]
                zb[s % 8, 8 * (s // 8) : 8 * (s // 8) + 8] = acc_t[18 * s + 10 : 18 * s + 18]

    pass_on(0)
    pass_on(1)
    pass_core(0)
    pass_on(2)
    for s in range(8):
        halo[s].wait_recv()
    project(0)
    pass_core(1)
    attend(0)
    project(1)
    pass_core(2)
    attend(1)
    project(2)
    attend(2)
    write_att = pltpu.make_async_copy(att_ref, att_hbm, out_sem.at[0])
    write_att.start()
    acc[:, 96:128, :] = jnp.zeros((3, 32, 384), F32)
    ta[80:88] = jnp.zeros((8, 128), F32)
    tokens_out.wait_recv()
    finish(0)
    cross_send(0, 0)
    cross_send(1, 0)
    finish(1)
    cross_send(0, 1)
    cross_send(2, 0)
    cross_send(1, 1)
    finish(2)
    cross_sum(0, 0)
    cross_sum(1, 0)
    cross_send(2, 1)
    grad_tokens = dot_nt(gq[0, 0:256], wp[0]) + dot_nt(gq[1, 0:256], wp[1]) + dot_nt(gq[2, 0:256], wp[2])
    gtok_ref[...] = grad_tokens.astype(BF16)
    write_gtok = pltpu.make_async_copy(gtok_ref, gtok_hbm, out_sem.at[1])
    write_gtok.start()
    cross_sum(0, 1)
    cross_sum(2, 0)
    cross_sum(1, 1)
    cross_sum(2, 1)

    sya[...] = ya[...].astype(BF16)
    szb[...] = zb[...].astype(BF16)
    last = {}
    order = (4, 3, 5, 2, 6, 1, 7)
    for d in order:
        last["ya", d] = remote(
            sya.at[(y + d) % 8], rya.at[d - 1], ya_send.at[d - 1], ya_recv.at[d - 1], y_peer[d]
        )
        last["zb", d] = remote(
            szb.at[(z + d) % 8], rzb.at[d - 1], zb_send.at[d - 1], zb_recv.at[d - 1], z_peer[d]
        )
        last["ya", d].start()
        last["zb", d].start()
    total = zb[z]
    for d in reversed(order):
        last["zb", d].wait_recv()
        total += rzb[d - 1].astype(F32)
    for n in range(8):
        tb[n] = total[8 * n : 8 * n + 8]
    for d in order:
        last["yb", d] = remote(
            tb.at[(y + d) % 8], ryb.at[d - 1], yb_send.at[d - 1], yb_recv.at[d - 1], y_peer[d]
        )
        last["yb", d].start()
    total = ya[y]
    for d in reversed(order):
        last["ya", d].wait_recv()
        total += rya[d - 1].astype(F32)
    ta[0:80] = total
    for n in range(8):
        sza[n] = ta[10 * n : 10 * n + 16]
    for d in order:
        last["za", d] = remote(
            sza.at[(z + d) % 8], rza.at[d - 1], za_send.at[d - 1], za_recv.at[d - 1], z_peer[d]
        )
        last["za", d].start()
    total_b = tb[y]
    for d in reversed(order):
        last["yb", d].wait_recv()
        total_b += ryb[d - 1]
    total_a = sza[z]
    for d in reversed(order):
        last["za", d].wait_recv()
        total_a += rza[d - 1]
    fin[0:16] = total_a * (1.0 / 8.0)
    fin[10:18] = total_b * (1.0 / 8.0)
    out_ref[...] = fin[0:18, 0:96]

    started = list(wx.values()) + list(wc.values()) + list(halo.values()) + list(back.values())
    started += list(core.values()) + list(cross.values()) + list(last.values()) + [tokens_out]
    for copy in started:
        copy.wait_send()
    write_att.wait()
    write_gtok.wait()


def local(tokens, w_qkv, score_scale, grad_out):
    dma = pltpu.SemaphoreType.DMA
    vmem = pl.BlockSpec(memory_space=pltpu.VMEM)
    anywhere = pl.BlockSpec(memory_space=pl.ANY)
    shapes = (
        jax.ShapeDtypeStruct((256, 384), BF16),
        jax.ShapeDtypeStruct((256, 768), BF16),
        jax.ShapeDtypeStruct((18, 96), F32),
    )
    attended, grad_tokens, weight_grad = pl.pallas_call(
        kernel,
        out_shape=shapes,
        in_specs=[anywhere] * 4,
        out_specs=(anywhere, anywhere, vmem),
        scratch_shapes=[
            pltpu.VMEM((512, 768), BF16),
            pltpu.VMEM((256, 384), BF16),
            pltpu.SMEM((6,), F32),
            pltpu.VMEM((256, 384), BF16),
            pltpu.VMEM((256, 768), BF16),
            pltpu.VMEM((3, 768, 384), BF16),
            pltpu.VMEM((4, 2, 96, 256), BF16),
            pltpu.VMEM((4, 96, 512), BF16),
            pltpu.VMEM((512, 256), F32),
            pltpu.VMEM((256, 256), BF16),
            pltpu.VMEM((256, 256), BF16),
            pltpu.VMEM((3, 256, 256), BF16),
            pltpu.VMEM((3, 256, 256), F32),
            pltpu.VMEM((3, 2, 256, 128), BF16),
            pltpu.VMEM((3, 2, 256, 128), BF16),
            pltpu.VMEM((3, 512, 256), BF16),
            pltpu.VMEM((256, 768), BF16),
            pltpu.VMEM((3, 256, 256), F32),
            pltpu.VMEM((3, 256, 256), BF16),
            pltpu.VMEM((3, 256, 256), BF16),
            pltpu.VMEM((3, 512, 384), BF16),
            pltpu.VMEM((3, 3, 96, 384), BF16),
            pltpu.VMEM((3, 3, 96, 384), BF16),
            pltpu.VMEM((3, 128, 384), F32),
            pltpu.VMEM((1152, 128), F32),
            pltpu.VMEM((8, 80, 128), F32),
            pltpu.VMEM((8, 64, 128), F32),
            pltpu.VMEM((8, 80, 128), BF16),
            pltpu.VMEM((8, 64, 128), BF16),
            pltpu.VMEM((7, 80, 128), BF16),
            pltpu.VMEM((7, 64, 128), BF16),
            pltpu.VMEM((88, 128), F32),
            pltpu.VMEM((8, 8, 128), F32),
            pltpu.VMEM((8, 16, 128), F32),
            pltpu.VMEM((7, 16, 128), F32),
            pltpu.VMEM((7, 8, 128), F32),
            pltpu.VMEM((24, 128), F32),
            dma((3,)), dma((3, 3)), dma((2,)), dma((3, 4)), dma((3, 4)), dma((3, 5)), dma((3, 5)),
            dma((8,)), dma((8,)), dma((3, 8)), dma((3, 8)),
            dma, dma, dma((3, 2)), dma((3, 2)), dma((3, 2, 3)), dma((3, 2, 3)),
            dma((7,)), dma((7,)), dma((7,)), dma((7,)), dma((7,)), dma((7,)), dma((7,)), dma((7,)),
        ],
        compiler_params=pltpu.CompilerParams(
            collective_id=0, has_side_effects=True, vmem_limit_bytes=63 * 1024 * 1024
        ),
    )(tokens.reshape(256, 768), w_qkv, score_scale, grad_out.reshape(256, 384))
    return (
        attended.reshape(1, 1, 16, 16, 384),
        grad_tokens.reshape(1, 1, 16, 16, 768),
        weight_grad.T,
    )


def solution(mesh):
    return jax.shard_map(
        local,
        mesh=mesh,
        in_specs=(
            P("img", "sp", None, None, None),
            P("img", None),
            P(),
            P("img", "sp", None, None, None),
        ),
        out_specs=(
            P("img", "sp", None, None, None),
            P("img", "sp", None, None, None),
            P("img", "sp"),
        ),
        check_vma=False,
    )
```

time: 71.4 us -> 60.2 us (0.84)
  Pallas kernels: 64.7 us -> 56.4 us
  local copies, waits for them, and re-layouts: 5.61 us -> 3.03 us
    pallas_call x1, Pallas kernels: 64.7 us -> 56.4 us  [local(): pl.pallas_call(kernel, out_shape=shapes, in_specs=[anywhere] * 4, out_spe...]
    unnamed x11 -> x7, local copies, waits for them, and re-layouts: 5.61 us -> 3.03 us
where the time goes in v3:
time: 60.2 us; the launch traced here: 60 us
  Pallas kernels  56.4 us (94%)
  local copies, waits for them, and re-layouts  3.03 us (5%)
  between operations  0.65 us (1%)
    pallas_call x1, Pallas kernels, local(): pl.pallas_call(kernel, out_shape=shapes, in_specs=[anywhere] * 4, out_spe...  56.4 us
    unnamed x7, local copies, waits for them, and re-layouts  3.03 us

profile of v3, /device:TPU:1, one launch (start us, length us, event | category | flops | bytes accessed | tf_op | source)
XLA Modules:
  0.0 60.0 jit_solution(9391371426993823683)
XLA Ops:
  0.6 56.4 %shard_map.67 = (bf16[256,384]{1,0:T(8,128)(2,1)}, bf16[256,768]{1,0:T(8,128)(2,1)}, f32[18,96]{1,0:T(8,128)}) custom-call(bf16[256,768]{1,0:T(8,128)(2,1)} %bitcast.6, bf16[96,1152]{1,0:T(8,128)(2,1)} %w_hbm.1, f32[6]{0:T(128)} %scale_hbm.1, bf16[256,384]{1,0:T(8,128)(2,1)} %bitcast.8), custom_call_target="tpu_custom_call" | custom-call | tf_op jit(solution)/shard_map/pallas_call | solution.py:444
  57.0 0.0 copy-start
  57.0 1.7 %copy.10 = bf16[1,1,16,16,384]{4,3,2,1,0:T(8,128)(2,1)} copy(bf16[1,1,16,16,384]{4,3,2,1,0:T(8,128)(2,1)} %bitcast.7) | data formatting | bytes 393216
  58.7 0.0 copy-done
  58.7 0.0 copy-start.1
  58.7 0.7 %copy.11 = bf16[1,1,16,16,768]{4,3,2,1,0:T(8,128)(2,1)} copy(bf16[1,1,16,16,768]{4,3,2,1,0:T(8,128)(2,1)S(1)} %bitcast.5) | data formatting | bytes 786432
  59.4 0.0 copy-done.1
  59.4 0.6 copy.12
Async XLA Ops:
  57.0 1.7 %copy-start = (bf16[256,768]{1,0:T(8,128)(2,1)S(1)}, bf16[256,768]{1,0:T(8,128)(2,1)}, u32[]{:S(2)}) copy-start(bf16[256,768]{1,0:T(8,128)(2,1)} %get-tuple-element.7) | copy-start | bytes 1179652
  58.7 0.8 %copy-start.1 = (f32[18,96]{1,0:T(8,128)S(1)}, f32[18,96]{1,0:T(8,128)}, u32[]{:S(2)}) copy-start(f32[18,96]{1,0:T(8,128)} %get-tuple-element.8) | copy-start | bytes 20740

commit v4 on v3

--- a/solution.py
+++ b/solution.py
@@ -96,12 +96,6 @@
     def tile_at(rstep, cstep):
         return (img, 8 * ((y + rstep + 8) % 8) + (z + cstep + 8) % 8)
 
-    barrier = pltpu.get_barrier_semaphore()
-    peers = [other_core] + x_peer[1:] + y_peer[1:] + z_peer[1:]
-    peers += [tile_at(r, s) for r in (-1, 1) for s in (-1, 1)]
-    for peer in peers:
-        pl.semaphore_signal(barrier, inc=1, device_id=peer, device_id_type=MESH)
-
     def block(b):
         return pl.ds(pl.multiple_of(96 * b, 32), 96)
 
@@ -119,56 +113,62 @@
         for p in range(3)
         for part in range(3)
     ]
-    for load in w_loads + loads:
+    barrier = pltpu.get_barrier_semaphore()
+    peers = [other_core] + x_peer[1:] + y_peer[1:] + z_peer[1:]
+    peers += [tile_at(r, s) for r in (-1, 1) for s in (-1, 1)]
+    for peer in peers[:4]:
+        pl.semaphore_signal(barrier, inc=1, device_id=peer, device_id_type=MESH)
+    for load in w_loads + loads[:1]:
         load.start()
-    query = lax.broadcasted_iota(jnp.int32, (1, 256), 1)
-    query_row, query_col = query >> 4, query & 15
-
-    def put_bias(low, key_row, key_col):
-        near = (jnp.abs(key_row - query_row) <= 3) & (jnp.abs(key_col - query_col) <= 3)
-        bias[low : low + 256] = jnp.where(near, 0.0, NEVER).astype(F32)
+    for peer in peers[4:]:
+        pl.semaphore_signal(barrier, inc=1, device_id=peer, device_id_type=MESH)
+    for load in loads[1:]:
+        load.start()
+
+    for load in w_loads:
+        load.wait()
+    pl.semaphore_wait(barrier, len(peers))
+
+    wx, wc = {}, {}
+
+    def to_core(p, n, ref):
+        wc[p, n] = remote(ref, ref, wc_send.at[p, n], wc_recv.at[p, n], other_core)
+        wc[p, n].start()
+
+    def to_x(p, n, ref, d):
+        wx[p, n] = remote(ref, ref, wx_send.at[p, n], wx_recv.at[p, n], x_peer[d])
+        wx[p, n].start()
+
+    def half(b, h):
+        return pl.ds(pl.multiple_of(96 * b + 48 * h, 16), 48)
+
+    left, right, across = [2 * ((x + d) % 4) + c for d in (3, 1, 2)]
+
+    def share(p):
+        mine = wp.at[p, block(img)]
+        to_x(p, 2, mine, 2)
+        to_x(p, 0, mine, 1)
+        to_x(p, 1, mine, 3)
+        to_core(p, 0, mine)
+
+    def pass_on(p):
+        wx[p, 0].wait_recv()
+        to_core(p, 1, wp.at[p, block(left)])
+        wx[p, 1].wait_recv()
+        to_core(p, 2, wp.at[p, block(right)])
+
+    def pass_core(p):
+        wx[p, 2].wait_recv()
+        to_core(p, 3, wp.at[p, block(across)])
+
+    for p in range(3):
+        share(p)
 
     j_rows = lax.broadcasted_iota(jnp.int32, (256, 1), 0)
-    put_bias(0, j_rows >> 4, j_rows & 15)
-    row, col, _, _, filled = halo_place(j_rows)
-    grow, gcol = row + 16 * y, col + 16 * z
-    inside = filled & (grow >= 0) & (grow < 128) & (gcol >= 0) & (gcol < 128)
-    put_bias(256, jnp.where(inside, row, 1000), col)
     j_cols = lax.broadcasted_iota(jnp.int32, (1, 256), 1)
     wide_rows = lax.broadcasted_iota(jnp.int32, (256, 256), 0)
     wide_cols = lax.broadcasted_iota(jnp.int32, (256, 256), 1)
     pack[...] = jnp.where(owner_token(j_rows) == wide_cols, 1.0, 0.0).astype(BF16)
-    unpack[...] = jnp.where(owner_token(j_cols) == wide_rows, 1.0, 0.0).astype(BF16)
-    lane_r = lax.broadcasted_iota(jnp.int32, (128, 128), 0)
-    lane_c = lax.broadcasted_iota(jnp.int32, (128, 128), 1)
-    same_head = jnp.where((lane_r >> 6) == (lane_c >> 6), 1.0, 0.0).astype(BF16)
-    eye = jnp.where(lane_r == lane_c, 1.0, 0.0).astype(BF16)
-    lane = lax.broadcasted_iota(jnp.int32, (1, 128), 1)
-    head_mask = [jnp.where((lane >> 6) == e, 1.0, 0.0).astype(F32) for e in range(2)]
-
-    for load in w_loads:
-        load.wait()
-    pl.semaphore_wait(barrier, len(peers))
-
-    wx, wc = {}, {}
-
-    def to_core(p, n, ref):
-        wc[p, n] = remote(ref, ref, wc_send.at[p, n], wc_recv.at[p, n], other_core)
-        wc[p, n].start()
-
-    def to_x(p, n, ref, d):
-        wx[p, n] = remote(ref, ref, wx_send.at[p, n], wx_recv.at[p, n], x_peer[d])
-        wx[p, n].start()
-
-    def half(b, h):
-        return pl.ds(pl.multiple_of(96 * b + 48 * h, 16), 48)
-
-    left, right, across = [2 * ((x + d) % 4) + c for d in (3, 1, 2)]
-    for p in range(3):
-        mine = wp.at[p, block(img)]
-        to_x(p, 0, mine, 1)
-        to_x(p, 1, mine, 3)
-        to_core(p, 0, mine)
 
     for load in loads:
         load.wait()
@@ -184,18 +184,25 @@
         )
         halo[s].start()
 
-    def pass_on(p):
-        wx[p, 0].wait_recv()
-        to_x(p, 2, wp.at[p, half(left, 0)], 1)
-        to_core(p, 1, wp.at[p, block(left)])
-        wx[p, 1].wait_recv()
-        to_x(p, 3, wp.at[p, half(right, 1)], 3)
-        to_core(p, 2, wp.at[p, block(right)])
-
-    def pass_core(p):
-        for h in range(2):
-            wx[p, 2 + h].wait_recv()
-            to_core(p, 3 + h, wp.at[p, half(across, h)])
+    query = lax.broadcasted_iota(jnp.int32, (1, 256), 1)
+    query_row, query_col = query >> 4, query & 15
+
+    def put_bias(low, key_row, key_col):
+        near = (jnp.abs(key_row - query_row) <= 3) & (jnp.abs(key_col - query_col) <= 3)
+        bias[low : low + 256] = jnp.where(near, 0.0, NEVER).astype(F32)
+
+    put_bias(0, j_rows >> 4, j_rows & 15)
+    row, col, _, _, filled = halo_place(j_rows)
+    grow, gcol = row + 16 * y, col + 16 * z
+    inside = filled & (grow >= 0) & (grow < 128) & (gcol >= 0) & (gcol < 128)
+    put_bias(256, jnp.where(inside, row, 1000), col)
+    unpack[...] = jnp.where(owner_token(j_cols) == wide_rows, 1.0, 0.0).astype(BF16)
+    lane_r = lax.broadcasted_iota(jnp.int32, (128, 128), 0)
+    lane_c = lax.broadcasted_iota(jnp.int32, (128, 128), 1)
+    same_head = jnp.where((lane_r >> 6) == (lane_c >> 6), 1.0, 0.0).astype(BF16)
+    eye = jnp.where(lane_r == lane_c, 1.0, 0.0).astype(BF16)
+    lane = lax.broadcasted_iota(jnp.int32, (1, 128), 1)
+    head_mask = [jnp.where((lane >> 6) == e, 1.0, 0.0).astype(F32) for e in range(2)]
 
     for p in range(3):
         g_pair = g_ref[:, 128 * p : 128 * p + 128].astype(F32)
@@ -209,6 +216,8 @@
     )
     tokens_out.start()
     tok_2[:, :, 0:256] = tok_t[:, c]
+    acc[:, 96:128, :] = jnp.zeros((3, 32, 384), F32)
+    ta[80:88] = jnp.zeros((8, 128), F32)
 
     def head_sum(v):
         high = v.astype(BF16)
@@ -228,8 +237,8 @@
         core[p, n].start()
 
     def project(p):
-        for n in range(5):
-            wc[p, n].wait_recv()
+        for d in range(4):
+            wc[p, d].wait_recv()
         low = dot(tokx[0:256], wp[p]).astype(BF16)
         far = dot(tokx[256:512], wp[p, :, 128:384]).astype(BF16)
         qk[p] = low[:, 0:256]
@@ -252,41 +261,47 @@
     def attend(p):
         key = kvx[p, :, 0:128]
         value = kvx[p, :, 128:256]
-        key_t = dot_nt(eye, key).astype(BF16)
-        value_t = dot_nt(eye, value).astype(BF16)
-        att_t, gq_t = [], []
-        grad_k, grad_v = None, None
+        lows, grads = [], []
         for e in range(2):
             scale = scale_ref[2 * p + e]
-            rows = slice(64 * e, 64 * e + 64)
             raised = jnp.exp(dot_nt(key, qum[p, e]) * scale + bias[...])
             attention = raised * (1.0 / jnp.sum(raised, axis=0, keepdims=True))
-            att_low = attention.astype(BF16)
             grad_att = dot_nt(value, gm[p, e])
             row_total = jnp.sum(attention * grad_att, axis=0, keepdims=True)
-            grad_s = (attention * scale * (grad_att - row_total)).astype(BF16)
-            att_t.append(dot(value_t[rows], att_low))
-            gq_t.append(dot(key_t[rows], grad_s))
-            grad_v_e = dot(att_low, gm[p, e])
-            grad_k_e = dot(grad_s, qum[p, e])
-            grad_v = grad_v_e if grad_v is None else grad_v + grad_v_e
-            grad_k = grad_k_e if grad_k is None else grad_k + grad_k_e
-        ghs[p, :, 0:128] = grad_k[256:512].astype(BF16)
-        ghs[p, :, 128:256] = grad_v[256:512].astype(BF16)
-        for s, (rstep, cstep, first, rows) in enumerate(STRIPS):
+            lows.append(attention.astype(BF16))
+            grads.append((attention * scale * (grad_att - row_total)).astype(BF16))
+
+        def key_side(first):
+            rows = slice(first, first + 256)
+            grad_k = dot(grads[0][rows], qum[p, 0]) + dot(grads[1][rows], qum[p, 1])
+            grad_v = dot(lows[0][rows], gm[p, 0]) + dot(lows[1][rows], gm[p, 1])
+            return grad_k, grad_v
+
+        grad_k, grad_v = key_side(256)
+        ghs[p, :, 0:128] = grad_k.astype(BF16)
+        ghs[p, :, 128:256] = grad_v.astype(BF16)
+        for s, (rstep, cstep, first, rows) in reversed(list(enumerate(STRIPS))):
             span = pl.ds(first, rows)
             back[p, s] = remote(
                 ghs.at[p, span], ghr.at[p, span], gh_send.at[p, s], gh_recv.at[p, s], tile_at(rstep, cstep)
             )
             back[p, s].start()
-        own[p, :, 0:128] = grad_k[0:256]
-        own[p, :, 128:256] = grad_v[0:256]
-        att_ref[:, 128 * p : 128 * p + 128] = jnp.concatenate(att_t, axis=0).T.astype(BF16)
+        key_t = dot_nt(eye, key).astype(BF16)
+        value_t = dot_nt(eye, value).astype(BF16)
+        att_t, gq_t = [], []
+        for e in range(2):
+            rows = slice(64 * e, 64 * e + 64)
+            gq_t.append(dot(key_t[rows], grads[e]))
+            att_t.append(dot(value_t[rows], lows[e]))
         grad_q = jnp.concatenate(gq_t, axis=0).T
         q = qk[p, :, 0:128].astype(F32)
         inv_q = inv[p, :, 0:128]
         gq[p, 0:256, 0:128] = (inv_q * (grad_q - q * (inv_q * inv_q) * head_sum(grad_q * q))).astype(BF16)
         exchange(p, 0, pl.ds(0, 128))
+        grad_k, grad_v = key_side(0)
+        own[p, :, 0:128] = grad_k
+        own[p, :, 128:256] = grad_v
+        att_ref[:, 128 * p : 128 * p + 128] = jnp.concatenate(att_t, axis=0).T.astype(BF16)
 
     def finish(p):
         for s in range(8):
@@ -338,29 +353,27 @@
                 zb[s % 8, 8 * (s // 8) : 8 * (s // 8) + 8] = acc_t[18 * s + 10 : 18 * s + 18]
 
     pass_on(0)
-    pass_on(1)
     pass_core(0)
-    pass_on(2)
     for s in range(8):
         halo[s].wait_recv()
     project(0)
+    attend(0)
+    pass_on(1)
     pass_core(1)
-    attend(0)
     project(1)
+    tokens_out.wait_recv()
+    cross_send(0, 0)
+    attend(1)
+    pass_on(2)
     pass_core(2)
-    attend(1)
+    finish(0)
+    cross_send(1, 0)
     project(2)
     attend(2)
     write_att = pltpu.make_async_copy(att_ref, att_hbm, out_sem.at[0])
     write_att.start()
-    acc[:, 96:128, :] = jnp.zeros((3, 32, 384), F32)
-    ta[80:88] = jnp.zeros((8, 128), F32)
-    tokens_out.wait_recv()
-    finish(0)
-    cross_send(0, 0)
-    cross_send(1, 0)
+    cross_send(0, 1)
     finish(1)
-    cross_send(0, 1)
     cross_send(2, 0)
     cross_send(1, 1)
     finish(2)
@@ -484,7 +497,7 @@
             pltpu.VMEM((7, 16, 128), F32),
             pltpu.VMEM((7, 8, 128), F32),
             pltpu.VMEM((24, 128), F32),
-            dma((3,)), dma((3, 3)), dma((2,)), dma((3, 4)), dma((3, 4)), dma((3, 5)), dma((3, 5)),
+            dma((3,)), dma((3, 3)), dma((2,)), dma((3, 3)), dma((3, 3)), dma((3, 4)), dma((3, 4)),
             dma((8,)), dma((8,)), dma((3, 8)), dma((3, 8)),
             dma, dma, dma((3, 2)), dma((3, 2)), dma((3, 2, 3)), dma((3, 2, 3)),
             dma((7,)), dma((7,)), dma((7,)), dma((7,)), dma((7,)), dma((7,)), dma((7,)), dma((7,)),

time: 60.2 us -> 59 us (0.980)
  Pallas kernels: 56.4 us -> 55.2 us
    pallas_call x1, Pallas kernels: 56.4 us -> 55.2 us  [local(): pl.pallas_call(kernel, out_shape=shapes, in_specs=[anywhere] * 4, out_spe...]
where the time goes in v4:
time: 59 us; the launch traced here: 58.9 us
  Pallas kernels  55.2 us (94%)
  local copies, waits for them, and re-layouts  3.03 us (5%)
  between operations  0.65 us (1%)
    pallas_call x1, Pallas kernels, local(): pl.pallas_call(kernel, out_shape=shapes, in_specs=[anywhere] * 4, out_spe...  55.2 us
    unnamed x7, local copies, waits for them, and re-layouts  3.03 us

profile of v4, /device:TPU:1, one launch (start us, length us, event | category | flops | bytes accessed | tf_op | source)
XLA Modules:
  0.0 58.9 jit_solution(789513838928374766)
XLA Ops:
  0.6 55.2 %shard_map.67 = (bf16[256,384]{1,0:T(8,128)(2,1)}, bf16[256,768]{1,0:T(8,128)(2,1)}, f32[18,96]{1,0:T(8,128)}) custom-call(bf16[256,768]{1,0:T(8,128)(2,1)} %bitcast.6, bf16[96,1152]{1,0:T(8,128)(2,1)} %w_hbm.1, f32[6]{0:T(128)} %scale_hbm.1, bf16[256,384]{1,0:T(8,128)(2,1)} %bitcast.8), custom_call_target="tpu_custom_call" | custom-call | tf_op jit(solution)/shard_map/pallas_call | solution.py:457
  55.8 0.0 copy-start
  55.8 1.7 %copy.10 = bf16[1,1,16,16,384]{4,3,2,1,0:T(8,128)(2,1)} copy(bf16[1,1,16,16,384]{4,3,2,1,0:T(8,128)(2,1)} %bitcast.7) | data formatting | bytes 393216
  57.5 0.0 copy-done
  57.5 0.0 copy-start.1
  57.5 0.7 %copy.11 = bf16[1,1,16,16,768]{4,3,2,1,0:T(8,128)(2,1)} copy(bf16[1,1,16,16,768]{4,3,2,1,0:T(8,128)(2,1)S(1)} %bitcast.5) | data formatting | bytes 786432
  58.3 0.0 copy-done.1
  58.3 0.6 %copy.12 = f32[96,18]{0,1:T(8,128)} copy(f32[96,18]{0,1:T(8,128)S(1)} %bitcast.9) | data formatting | bytes 13824
Async XLA Ops:
  55.8 1.7 %copy-start = (bf16[256,768]{1,0:T(8,128)(2,1)S(1)}, bf16[256,768]{1,0:T(8,128)(2,1)}, u32[]{:S(2)}) copy-start(bf16[256,768]{1,0:T(8,128)(2,1)} %get-tuple-element.7) | copy-start | bytes 1179652
  57.5 0.8 %copy-start.1 = (f32[18,96]{1,0:T(8,128)S(1)}, f32[18,96]{1,0:T(8,128)}, u32[]{:S(2)}) copy-start(f32[18,96]{1,0:T(8,128)} %get-tuple-element.8) | copy-start | bytes 20740

commit v5 on v4

--- a/solution.py
+++ b/solution.py
@@ -387,24 +387,40 @@
     cross_sum(0, 1)
     cross_sum(2, 0)
     cross_sum(1, 1)
-    cross_sum(2, 1)
-
-    sya[...] = ya[...].astype(BF16)
-    szb[...] = zb[...].astype(BF16)
+
     last = {}
     order = (4, 3, 5, 2, 6, 1, 7)
     for d in order:
         last["ya", d] = remote(
             sya.at[(y + d) % 8], rya.at[d - 1], ya_send.at[d - 1], ya_recv.at[d - 1], y_peer[d]
         )
-        last["zb", d] = remote(
-            szb.at[(z + d) % 8], rzb.at[d - 1], zb_send.at[d - 1], zb_recv.at[d - 1], z_peer[d]
-        )
-        last["ya", d].start()
-        last["zb", d].start()
+        for h in range(2):
+            rows = pl.ds(32 * h, 32)
+            last["zb", h, d] = remote(
+                szb.at[(z + d) % 8, rows], rzb.at[d - 1, rows], zb_send.at[h, d - 1], zb_recv.at[h, d - 1], z_peer[d]
+            )
+
+    def waits_for_last(row):
+        return (row == 4) | (row == 5) | (row == 7)
+
+    sya[0:4] = ya[0:4].astype(BF16)
+    sya[6] = ya[6].astype(BF16)
+    szb[:, 0:32] = zb[:, 0:32].astype(BF16)
+    for d in order:
+        pl.when(jnp.logical_not(waits_for_last((y + d) % 8)))(last["ya", d].start)
+        last["zb", 0, d].start()
+    cross_sum(2, 1)
+
+    sya[4:6] = ya[4:6].astype(BF16)
+    sya[7] = ya[7].astype(BF16)
+    szb[:, 32:64] = zb[:, 32:64].astype(BF16)
+    for d in order:
+        pl.when(waits_for_last((y + d) % 8))(last["ya", d].start)
+        last["zb", 1, d].start()
     total = zb[z]
     for d in reversed(order):
-        last["zb", d].wait_recv()
+        last["zb", 0, d].wait_recv()
+        last["zb", 1, d].wait_recv()
         total += rzb[d - 1].astype(F32)
     for n in range(8):
         tb[n] = total[8 * n : 8 * n + 8]
@@ -419,7 +435,7 @@
         total += rya[d - 1].astype(F32)
     ta[0:80] = total
     for n in range(8):
-        sza[n] = ta[10 * n : 10 * n + 16]
+        sza[n] = ta[10 * n : 10 * n + 16].astype(BF16)
     for d in order:
         last["za", d] = remote(
             sza.at[(z + d) % 8], rza.at[d - 1], za_send.at[d - 1], za_recv.at[d - 1], z_peer[d]
@@ -429,10 +445,10 @@
     for d in reversed(order):
         last["yb", d].wait_recv()
         total_b += ryb[d - 1]
-    total_a = sza[z]
+    total_a = sza[z].astype(F32)
     for d in reversed(order):
         last["za", d].wait_recv()
-        total_a += rza[d - 1]
+        total_a += rza[d - 1].astype(F32)
     fin[0:16] = total_a * (1.0 / 8.0)
     fin[10:18] = total_b * (1.0 / 8.0)
     out_ref[...] = fin[0:18, 0:96]
@@ -493,14 +509,14 @@
             pltpu.VMEM((7, 64, 128), BF16),
             pltpu.VMEM((88, 128), F32),
             pltpu.VMEM((8, 8, 128), F32),
-            pltpu.VMEM((8, 16, 128), F32),
-            pltpu.VMEM((7, 16, 128), F32),
+            pltpu.VMEM((8, 16, 128), BF16),
+            pltpu.VMEM((7, 16, 128), BF16),
             pltpu.VMEM((7, 8, 128), F32),
             pltpu.VMEM((24, 128), F32),
             dma((3,)), dma((3, 3)), dma((2,)), dma((3, 3)), dma((3, 3)), dma((3, 4)), dma((3, 4)),
             dma((8,)), dma((8,)), dma((3, 8)), dma((3, 8)),
             dma, dma, dma((3, 2)), dma((3, 2)), dma((3, 2, 3)), dma((3, 2, 3)),
-            dma((7,)), dma((7,)), dma((7,)), dma((7,)), dma((7,)), dma((7,)), dma((7,)), dma((7,)),
+            dma((7,)), dma((7,)), dma((2, 7)), dma((2, 7)), dma((7,)), dma((7,)), dma((7,)), dma((7,)),
         ],
         compiler_params=pltpu.CompilerParams(
             collective_id=0, has_side_effects=True, vmem_limit_bytes=63 * 1024 * 1024

time: 59 us -> 58 us (0.983)
  Pallas kernels: 55.2 us -> 54.2 us
    pallas_call x1, Pallas kernels: 55.2 us -> 54.2 us  [local(): pl.pallas_call(kernel, out_shape=shapes, in_specs=[anywhere] * 4, out_spe...]
where the time goes in v5:
time: 58 us; the launch traced here: 57.9 us
  Pallas kernels  54.2 us (93%)
  local copies, waits for them, and re-layouts  3.03 us (5%)
  between operations  0.65 us (1%)
    pallas_call x1, Pallas kernels, local(): pl.pallas_call(kernel, out_shape=shapes, in_specs=[anywhere] * 4, out_spe...  54.2 us
    unnamed x7, local copies, waits for them, and re-layouts  3.03 us

profile of v5, /device:TPU:1, one launch (start us, length us, event | category | flops | bytes accessed | tf_op | source)
XLA Modules:
  0.0 57.9 jit_solution(6704614915016927788)
XLA Ops:
  0.6 54.2 %shard_map.67 = (bf16[256,384]{1,0:T(8,128)(2,1)}, bf16[256,768]{1,0:T(8,128)(2,1)}, f32[18,96]{1,0:T(8,128)}) custom-call(bf16[256,768]{1,0:T(8,128)(2,1)} %bitcast.6, bf16[96,1152]{1,0:T(8,128)(2,1)} %w_hbm.1, f32[6]{0:T(128)} %scale_hbm.1, bf16[256,384]{1,0:T(8,128)(2,1)} %bitcast.8), custom_call_target="tpu_custom_call" | custom-call | tf_op jit(solution)/shard_map/pallas_call | solution.py:473
  54.8 0.0 copy-start
  54.8 1.7 %copy.10 = bf16[1,1,16,16,384]{4,3,2,1,0:T(8,128)(2,1)} copy(bf16[1,1,16,16,384]{4,3,2,1,0:T(8,128)(2,1)} %bitcast.7) | data formatting | bytes 393216
  56.5 0.0 copy-done
  56.5 0.0 copy-start.1
  56.5 0.7 %copy.11 = bf16[1,1,16,16,768]{4,3,2,1,0:T(8,128)(2,1)} copy(bf16[1,1,16,16,768]{4,3,2,1,0:T(8,128)(2,1)S(1)} %bitcast.5) | data formatting | bytes 786432
  57.3 0.0 copy-done.1
  57.3 0.6 %copy.12 = f32[96,18]{0,1:T(8,128)} copy(f32[96,18]{0,1:T(8,128)S(1)} %bitcast.9) | data formatting | bytes 13824
Async XLA Ops:
  54.8 1.7 %copy-start = (bf16[256,768]{1,0:T(8,128)(2,1)S(1)}, bf16[256,768]{1,0:T(8,128)(2,1)}, u32[]{:S(2)}) copy-start(bf16[256,768]{1,0:T(8,128)(2,1)} %get-tuple-element.7) | copy-start | bytes 1179652
  56.5 0.8 %copy-start.1 = (f32[18,96]{1,0:T(8,128)S(1)}, f32[18,96]{1,0:T(8,128)}, u32[]{:S(2)}) copy-start(f32[18,96]{1,0:T(8,128)} %get-tuple-element.8) | copy-start | bytes 20740

commit v6 on v5

--- a/solution.py
+++ b/solution.py
@@ -125,6 +125,12 @@
     for load in loads[1:]:
         load.start()
 
+    j_rows = lax.broadcasted_iota(jnp.int32, (256, 1), 0)
+    j_cols = lax.broadcasted_iota(jnp.int32, (1, 256), 1)
+    wide_rows = lax.broadcasted_iota(jnp.int32, (256, 256), 0)
+    wide_cols = lax.broadcasted_iota(jnp.int32, (256, 256), 1)
+    pack[...] = jnp.where(owner_token(j_rows) == wide_cols, 1.0, 0.0).astype(BF16)
+
     for load in w_loads:
         load.wait()
     pl.semaphore_wait(barrier, len(peers))
@@ -163,12 +169,6 @@
 
     for p in range(3):
         share(p)
-
-    j_rows = lax.broadcasted_iota(jnp.int32, (256, 1), 0)
-    j_cols = lax.broadcasted_iota(jnp.int32, (1, 256), 1)
-    wide_rows = lax.broadcasted_iota(jnp.int32, (256, 256), 0)
-    wide_cols = lax.broadcasted_iota(jnp.int32, (256, 256), 1)
-    pack[...] = jnp.where(owner_token(j_rows) == wide_cols, 1.0, 0.0).astype(BF16)
 
     for load in loads:
         load.wait()

time: 58 us -> 58 us (level)
  no operation moved by 1% of the time
where the time goes in v6:
time: 58 us; the launch traced here: 57.9 us
  Pallas kernels  54.2 us (93%)
  local copies, waits for them, and re-layouts  3.03 us (5%)
  between operations  0.65 us (1%)
    pallas_call x1, Pallas kernels, local(): pl.pallas_call(kernel, out_shape=shapes, in_specs=[anywhere] * 4, out_spe...  54.2 us
    unnamed x7, local copies, waits for them, and re-layouts  3.03 us

profile of v6, /device:TPU:1, one launch (start us, length us, event | category | flops | bytes accessed | tf_op | source)
XLA Modules:
  0.0 57.9 jit_solution(18112998079935907591)
XLA Ops:
  0.6 54.2 %shard_map.67 = (bf16[256,384]{1,0:T(8,128)(2,1)}, bf16[256,768]{1,0:T(8,128)(2,1)}, f32[18,96]{1,0:T(8,128)}) custom-call(bf16[256,768]{1,0:T(8,128)(2,1)} %bitcast.6, bf16[96,1152]{1,0:T(8,128)(2,1)} %w_hbm.1, f32[6]{0:T(128)} %scale_hbm.1, bf16[256,384]{1,0:T(8,128)(2,1)} %bitcast.8), custom_call_target="tpu_custom_call" | custom-call | tf_op jit(solution)/shard_map/pallas_call | solution.py:473
  54.8 0.0 copy-start
  54.9 1.7 %copy.10 = bf16[1,1,16,16,384]{4,3,2,1,0:T(8,128)(2,1)} copy(bf16[1,1,16,16,384]{4,3,2,1,0:T(8,128)(2,1)} %bitcast.7) | data formatting | bytes 393216
  56.5 0.0 copy-done
  56.5 0.0 copy-start.1
  56.5 0.7 %copy.11 = bf16[1,1,16,16,768]{4,3,2,1,0:T(8,128)(2,1)} copy(bf16[1,1,16,16,768]{4,3,2,1,0:T(8,128)(2,1)S(1)} %bitcast.5) | data formatting | bytes 786432
  57.3 0.0 copy-done.1
  57.3 0.6 %copy.12 = f32[96,18]{0,1:T(8,128)} copy(f32[96,18]{0,1:T(8,128)S(1)} %bitcast.9) | data formatting | bytes 13824
Async XLA Ops:
  54.8 1.7 %copy-start = (bf16[256,768]{1,0:T(8,128)(2,1)S(1)}, bf16[256,768]{1,0:T(8,128)(2,1)}, u32[]{:S(2)}) copy-start(bf16[256,768]{1,0:T(8,128)(2,1)} %get-tuple-element.7) | copy-start | bytes 1179652
  56.5 0.8 %copy-start.1 = (f32[18,96]{1,0:T(8,128)S(1)}, f32[18,96]{1,0:T(8,128)}, u32[]{:S(2)}) copy-start(f32[18,96]{1,0:T(8,128)} %get-tuple-element.8) | copy-start | bytes 20740
